TPU v7x, 512 devices: a whole 4x4x16 slice. The times are simulated.
512 devices in a mesh: fsdp: 32 (over x, y, core), tx: 4 (over z_hi), ty: 4 (over z_lo).
Axes of the slice: x: 4, y: 4, z: 16 (z_hi: 4, z_lo: 4; z = z_hi * 4 + z_lo), core: 2. Of those that a mesh axis runs over, the one named last changes fastest.
Arguments:
- context: bfloat16 [32768, 4096], P('fsdp', ('tx', 'ty')), may hold values from -6 to 6
- residual: bfloat16 [32768, 8192], P('fsdp', ('ty', 'tx')), may hold values from -30 to 30
- policy_weight: bfloat16 [8192, 4096], P(('ty', 'fsdp'), 'tx'), may hold values from -0.09375 to 0.09375
- master_weight: float32 [8192, 4096], P(('ty', 'fsdp'), 'tx'), may hold values from -0.09375 to 0.09375
- norm_gain: bfloat16 [8192], P(('ty', 'tx')), may hold values from 0.099609375 to 1.8984375
Outputs:
- normed: bfloat16 [32768, 8192], P('fsdp', ('ty', 'tx'))
- new_master: float32 [8192, 4096], P(('ty', 'fsdp'), 'tx')
All inputs are finite; a program needn't handle non-finite values.
Results may differ from a plain program's by a relative error of at most 0.013.
Values may be sent and summed in bfloat16 or wider, within the bound.
No kernel may reach another device: no remote copies, remote signals or barrier semaphores. Data moves between devices by JAX's collectives and lax.ppermute only.
A program may use at most 64 MiB of HBM per device.

v0:
```python
import jax
import jax.numpy as jnp
from jax import lax
from jax.sharding import PartitionSpec as P

D = 8192


mix_rate = 0.6


def on_whole(value, axis, dim, block):
    whole = lax.all_gather(value, axis, axis=dim, tiled=True)
    return block(whole, jnp.int32(0))


def shards(context, residual, policy_weight, master_weight, norm_gain):
    new_master = mix_rate * policy_weight.astype(jnp.float32) + (1.0 - mix_rate) * master_weight
    context_block = lax.all_gather(context, "ty", axis=1, tiled=True)

    def project(shard_rows):
        return lax.dot_general(
            context_block, shard_rows, (((1,), (1,)), ((), ())), preferred_element_type=jnp.float32
        )

    def project_mixed(shard_pair):
        policy_piece, master_piece = shard_pair
        mixed_piece = (
            mix_rate * policy_piece.astype(jnp.float32) + (1.0 - mix_rate) * master_piece
        ).astype(jnp.bfloat16)
        return project(mixed_piece)

    partials = on_whole(
        (policy_weight, master_weight.astype(jnp.bfloat16)),
        "fsdp",
        0,
        lambda piece, start: project_mixed((piece[0], piece[1].astype(jnp.float32))),
    )
    summed = lax.psum_scatter(
        partials.astype(jnp.bfloat16), "tx", scatter_dimension=1, tiled=True
    ).astype(jnp.float32)
    hidden = residual.astype(jnp.float32) + summed
    totals = lax.psum(jnp.sum(hidden * hidden, axis=1), ("tx", "ty"))
    square_mean = (totals / D)[:, None]
    normed = (
        hidden * lax.rsqrt(square_mean + 1e-05) * norm_gain.astype(jnp.float32)[None, :]
    ).astype(jnp.bfloat16)
    return (normed, new_master)


def solution(mesh):
    return jax.shard_map(
        shards,
        mesh=mesh,
        in_specs=(
            P("fsdp", ("tx", "ty")),
            P("fsdp", ("ty", "tx")),
            P(("ty", "fsdp"), "tx"),
            P(("ty", "fsdp"), "tx"),
            P(("ty", "tx")),
        ),
        out_specs=(P("fsdp", ("ty", "tx")), P(("ty", "fsdp"), "tx")),
        check_vma=False,
    )
```

profile of v0, /device:TPU:6, one launch (start us, length us, event | category | flops | bytes accessed | tf_op | source)
XLA Modules:
  0.0 409.6 jit_solution(18137988367590792427)
XLA Ops:
  7.2 0.0 all-gather.8.cloned.1.call-start
  7.2 0.7 all-gather.8.cloned.1.call-update
  7.9 0.0 all-gather.6.cloned.1.call-start
  7.9 1.9 multiply_add_fusion
  9.8 0.0 all-gather.6.cloned.1.call-update
  9.8 0.0 all-gather.4.cloned.1.call-start
  9.9 0.7 all-gather.4.cloned.1.call-update
  10.6 0.0 reduce-scatter.2.cloned.1.call-start
  10.6 60.3 %all-gather.8.cloned.1.call-done = bf16[1024,1024]{1,0:T(8,128)(2,1)} async-done(((bf16[1024,256]{1,0:T(8,128)(2,1)}), bf16[1024,1024]{1,0:T(8,128)(2,1)}) %all-gather.8.cloned.1.call-update) | async-done | bytes 2097168 | tf_op jit(solution)/shard_map/all_gather | solution.py:19
  71.0 63.1 %all-gather.6.cloned.1.call-done = bf16[2048,1024]{1,0:T(8,128)(2,1)} async-done(((bf16[64,1024]{1,0:T(8,128)(2,1)}), bf16[2048,1024]{1,0:T(8,128)(2,1)}) %all-gather.6.cloned.1.call-update) | async-done | bytes 4194320 | tf_op jit(solution)/shard_map/all_gather | solution.py:13
  134.1 64.0 %all-gather.4.cloned.1.call-done = bf16[2048,1024]{1,0:T(8,128)(2,1)} async-done(((bf16[64,1024]{1,0:T(8,128)(2,1)}), bf16[2048,1024]{1,0:T(8,128)(2,1)}) %all-gather.4.cloned.1.call-update) | async-done | bytes 4194320 | tf_op jit(solution)/shard_map/all_gather | solution.py:13
  198.1 10.6 %convert_bitcast_fusion = bf16[1024,2048]{0,1:T(8,128)(2,1)} fusion(bf16[1024,1024]{1,0:T(8,128)(2,1)} %all-gather.8.cloned.1.call-done, bf16[2048,1024]{1,0:T(8,128)(2,1)} %all-gather.6.cloned.1.call-done, bf16[2048,1024]{1,0:T(8,128)(2,1)} %all-gather.4.cloned.1.call-done), kind=kOutput, calls=%fused_computation.2 | convolution fusion | flops 4309647360 | bytes 14680064 | tf_op jit(solution)/shard_map/dot_general | solution.py:22
  208.7 0.0 copy-start
  208.7 0.0 copy-start.1
  208.7 0.0 reduce-scatter.2.cloned.1.call-update
  208.8 1.2 copy-done
  210.0 0.5 copy.7
  210.5 0.0 copy-done.1
  210.5 160.9 %reduce-scatter.2.cloned.1.call-done = bf16[1024,512]{0,1:T(8,128)(2,1)} async-done(((bf16[1024,2048]{0,1:T(8,128)(2,1)}), bf16[1024,512]{0,1:T(8,128)(2,1)}) %reduce-scatter.2.cloned.1.call-update) | async-done | bytes 1048592 | tf_op jit(solution)/shard_map/reduce_scatter | solution.py:39
  371.4 1.6 multiply_reduce_fusion
  373.1 27.0 %psum.7 = f32[1024]{0:T(1024)S(1)} all-reduce(f32[1024]{0:T(1024)S(1)} %multiply_reduce_fusion), channel_id=1, replica_groups=mesh['fsdp'=32,'tx'=4,'ty'=4] {'tx','ty'}, use_global_device_ids=true, to_apply=%region_2.0 | all-reduce | flops 1024 | bytes 8192 | tf_op jit(solution)/shard_map/psum | solution.py:43
  400.1 1.6 multiply_convert_fusion
  401.7 1.3 copy.8
  (2 shorter events, 0.0 us)
Async XLA Ops:
  7.2 63.8 %all-gather.8.cloned.1.call-start = ((), (), s32[]{:S(2)}) async-start(), calls=%async_computation.3 | async-start | bytes 2621440 | tf_op jit(solution)/shard_map/all_gather | solution.py:19
  7.9 126.2 %all-gather.6.cloned.1.call-start = ((), (), s32[]{:S(2)}) async-start(), calls=%async_computation.2 | async-start | bytes 4325376 | tf_op jit(solution)/shard_map/all_gather | solution.py:13
  9.8 188.3 %all-gather.4.cloned.1.call-start = ((), (), s32[]{:S(2)}) async-start(), calls=%async_computation.1 | async-start | bytes 4325376 | tf_op jit(solution)/shard_map/all_gather | solution.py:13
  10.6 360.9 %reduce-scatter.2.cloned.1.call-start = ((), (), s32[]{:S(2)}) async-start(), calls=%async_computation.4 | async-start | bytes 5242880 | tf_op jit(solution)/shard_map/reduce_scatter | solution.py:39
  208.7 1.2 copy-start
  208.7 1.8 copy-start.1
Sparse Core Ops, SparseCore 0:
  10.1 60.8 all-gather.7
  74.7 59.3 all-gather.5
  137.2 60.8 all-gather.3
  208.9 162.5 reduce-scatter.1
where the time goes:
time: 410 us
  waiting for transfers between devices  350 us (85%)
  blocking collectives  27 us (7%)
  between operations  13.8 us (3%)
  matrix products  10.6 us (3%)
  other arithmetic  5.11 us (1%)
    reduce_scatter x1, waiting for transfers between devices, shards(): lax.psum_scatter(partials.astype(jnp.bfloat16), 'tx', scatter_dimension=1...  161 us
    all_gather x2, waiting for transfers between devices, on_whole(): whole = lax.all_gather(value, axis, axis=dim, tiled=True)  127 us
    all_gather x1, waiting for transfers between devices, shards(): context_block = lax.all_gather(context, 'ty', axis=1, tiled=True)  60.3 us
    psum x1, blocking collectives, shards(): totals = lax.psum(jnp.sum(hidden * hidden, axis=1), ('tx', 'ty'))  27 us
    dot_general x1, matrix products, project(): lax.dot_general(context_block, shard_rows, (((1,), (1,)), ((), ())), pref...  10.6 us
  transfers between devices with their start and end apart: 4, of which 4 were waited for; matrix products, arithmetic and copies ran while one was open for 1% of the time, Pallas kernels for 0%

commit v1 on v0

v1 whole, which is shorter than its diff:
```python
import functools

import jax
import jax.numpy as jnp
from jax import lax
from jax.experimental import pallas as pl
from jax.experimental.pallas import tpu as pltpu
from jax.sharding import PartitionSpec as P

D = 8192
Z = ("tx", "ty")
NZ = 16

mix_rate = 0.6

TOK = 1024
FEAT = 256
COLS = 512
TILE = 256

UP = [(i, (i + 1) % NZ) for i in range(NZ)]
DOWN = [(i, (i - 1) % NZ) for i in range(NZ)]

SPREAD = []
LIFT = []
for u in range(4):
    for r in range(8):
        for t in range(4):
            s = (u - t) % 4
            SPREAD.append(((8 * u + r) * 4 + t, (4 * r + s) * 4 + t))
            LIFT.append(((4 * r + s) * 4 + t, (4 * r + s) * 4 + u))


def product_kernel(shifts, squares, z_ref, base_ref, weight_ref, *refs):
    blocks = refs[: len(shifts)]
    outs = refs[len(shifts) :]
    z = z_ref[0]
    total = base_ref[...].astype(jnp.float32)
    for shift, block in zip(shifts, blocks):
        source = lax.rem(z + (shift % NZ), NZ)
        turn = lax.rem(z // 4 - source // 4 + 4, 4)
        offset = pl.multiple_of(lax.rem(source, 4) * FEAT, FEAT)
        weight = weight_ref[:, turn, :, pl.ds(offset, FEAT)].reshape(COLS, FEAT)
        total += lax.dot_general(
            block[...], weight, (((1,), (1,)), ((), ())), preferred_element_type=jnp.float32
        )
    outs[0][...] = total
    if squares:
        ones = jnp.ones((8, COLS), jnp.float32)
        outs[1][...] = lax.dot_general(
            ones,
            total * total,
            (((1,), (1,)), ((), ())),
            precision=lax.Precision.HIGHEST,
            preferred_element_type=jnp.float32,
        )


def product(z, base, weight, shifts, blocks, squares):
    n = TOK // TILE
    whole = pl.BlockSpec((8, 4, 64, 1024), lambda i, z: (0, 0, 0, 0))
    out_shape = [jax.ShapeDtypeStruct((TOK, COLS), jnp.float32)]
    out_specs = [pl.BlockSpec((TILE, COLS), lambda i, z: (i, 0))]
    if squares:
        out_shape.append(jax.ShapeDtypeStruct((8, TOK), jnp.float32))
        out_specs.append(pl.BlockSpec((8, TILE), lambda i, z: (0, i)))
    return pl.pallas_call(
        functools.partial(product_kernel, shifts, squares),
        out_shape=out_shape,
        grid_spec=pltpu.PrefetchScalarGridSpec(
            num_scalar_prefetch=1,
            grid=(n,),
            in_specs=[pl.BlockSpec((TILE, COLS), lambda i, z: (i, 0)), whole]
            + [pl.BlockSpec((TILE, FEAT), lambda i, z: (i, 0))] * len(blocks),
            out_specs=out_specs,
        ),
        compiler_params=pltpu.CompilerParams(vmem_limit_bytes=40 * 1024 * 1024),
        cost_estimate=pl.CostEstimate(
            flops=2 * TOK * COLS * FEAT * len(blocks),
            bytes_accessed=4 * 1024 * 1024 + len(blocks) * TOK * FEAT * 2 + TOK * COLS * 8,
            transcendentals=0,
        ),
    )(z, base, weight, *blocks)


def shards(context, residual, policy_weight, master_weight, norm_gain):
    new_master = mix_rate * policy_weight.astype(jnp.float32) + (1.0 - mix_rate) * master_weight
    recast = new_master.astype(jnp.bfloat16)
    spread = lax.ppermute(recast, ("fsdp", "tx"), SPREAD)
    lifted = lax.ppermute(spread, ("fsdp", "tx"), LIFT)
    weight = lax.all_gather(lifted, "fsdp", axis=0).reshape(8, 4, 64, 1024)

    z = (lax.axis_index("tx") * 4 + lax.axis_index("ty")).astype(jnp.int32).reshape(1)
    below = above = context
    shifts, blocks = [0], [context]
    for step in range(1, 8):
        below = lax.ppermute(below, Z, UP)
        above = lax.ppermute(above, Z, DOWN)
        shifts += [-step, step]
        blocks += [below, above]
    half = TOK // 2
    far_low = lax.ppermute(below[:half], Z, UP)
    far_high = lax.ppermute(above[half:], Z, DOWN)
    far = jnp.concatenate([far_low, far_high], axis=0)

    (partial,) = product(z, residual, weight, shifts[:13], blocks[:13], False)
    hidden, squares = product(z, partial, weight, shifts[13:] + [8], blocks[13:] + [far], True)

    sent = jnp.broadcast_to(squares[:1], (NZ, TOK))
    totals = jnp.sum(lax.all_to_all(sent, Z, 0, 0, tiled=True), axis=0)
    square_mean = (totals / D)[:, None]
    normed = (
        hidden * lax.rsqrt(square_mean + 1e-05) * norm_gain.astype(jnp.float32)[None, :]
    ).astype(jnp.bfloat16)
    return (normed, new_master)


def solution(mesh):
    return jax.shard_map(
        shards,
        mesh=mesh,
        in_specs=(
            P("fsdp", ("tx", "ty")),
            P("fsdp", ("ty", "tx")),
            P(("ty", "fsdp"), "tx"),
            P(("ty", "fsdp"), "tx"),
            P(("ty", "tx")),
        ),
        out_specs=(P("fsdp", ("ty", "tx")), P(("ty", "fsdp"), "tx")),
        check_vma=False,
    )
```

time: 410 us -> 230 us (0.56)
  the two profiles are of different devices: /device:TPU:6 before, /device:TPU:14 now
where the time goes in v1:
time: 230 us; the launch traced here: 229 us
  waiting for transfers between devices  94.3 us (41%)
  starting transfers between devices  83.2 us (36%)
  local copies, waits for them, and re-layouts  23.9 us (10%)
  between operations  14.4 us (6%)
  Pallas kernels  9.23 us (4%)
  other arithmetic  4.11 us (2%)
    ppermute x7, waiting for transfers between devices, shards(): below = lax.ppermute(below, Z, UP)  49.4 us
    ppermute x7, starting transfers between devices, shards(): below = lax.ppermute(below, Z, UP)  27.1 us
    unnamed x60, local copies, waits for them, and re-layouts  23.2 us
    ppermute x7, starting transfers between devices, shards(): above = lax.ppermute(above, Z, DOWN)  21.5 us
    ppermute x1, starting transfers between devices, shards(): lifted = lax.ppermute(spread, ('fsdp', 'tx'), LIFT)  18.7 us
    ppermute x7, waiting for transfers between devices, shards(): above = lax.ppermute(above, Z, DOWN)  13.4 us
    all_to_all x1, waiting for transfers between devices, shards(): totals = jnp.sum(lax.all_to_all(sent, Z, 0, 0, tiled=True), axis=0)  12.8 us
    pallas_call x2, Pallas kernels, product(): pl.pallas_call(functools.partial(product_kernel, shifts, squares), out_sh...  9.23 us
  transfers between devices with their start and end apart: 20, of which 16 were waited for; matrix products, arithmetic and copies ran while one was open for 0% of the time, Pallas kernels for 0%

profile of v1, /device:TPU:14, one launch (start us, length us, event | category | flops | bytes accessed | tf_op | source)
XLA Modules:
  0.0 229.1 jit_solution(14003480952806166008)
XLA Ops:
  9.1 2.7 %collective-permute-start = (bf16[64,1024]{1,0:T(8,128)(2,1)S(1)}, bf16[64,1024]{1,0:T(8,128)(2,1)S(1)}, u32[]{:S(2)}, u32[]{:S(2)}) collective-permute-start(bf16[64,1024]{1,0:T(8,128)(2,1)S(1)} %get-tuple-element.6), channel_id=1, source_target_pairs={{0,0},{4,52},{8,40},{12,28},{16,64},{20,116},{24,104},{28,92},{32,... | collective-permute-start | bytes 393224 | tf_op jit(solution)/shard_map/ppermute | solution.py:89
  11.8 7.4 %collective-permute-done = bf16[64,1024]{1,0:T(8,128)(2,1)S(1)} collective-permute-done((bf16[64,1024]{1,0:T(8,128)(2,1)S(1)}, bf16[64,1024]{1,0:T(8,128)(2,1)S(1)}, u32[]{:S(2)}, u32[]{:S(2)}) %collective-permute-start) | collective-permute-done | bytes 131104 | tf_op jit(solution)/shard_map/ppermute | solution.py:89
  19.2 18.7 %collective-permute-start.1 = (bf16[64,1024]{1,0:T(8,128)(2,1)S(1)}, bf16[64,1024]{1,0:T(8,128)(2,1)S(1)}, u32[]{:S(2)}, u32[]{:S(2)}) collective-permute-start(bf16[64,1024]{1,0:T(8,128)(2,1)S(1)} %collective-permute-done), channel_id=1, source_target_pairs={{0,0},{52,48},{40,32},{28,16},{64,64},{116,112},{104,96},{92,80},{... | collective-permute-start | bytes 393224 | tf_op jit(solution)/shard_map/ppermute | solution.py:90
  38.0 4.3 %collective-permute-done.1 = bf16[64,1024]{1,0:T(8,128)(2,1)S(1)} collective-permute-done((bf16[64,1024]{1,0:T(8,128)(2,1)S(1)}, bf16[64,1024]{1,0:T(8,128)(2,1)S(1)}, u32[]{:S(2)}, u32[]{:S(2)}) %collective-permute-start.1) | collective-permute-done | bytes 131104 | tf_op jit(solution)/shard_map/ppermute | solution.py:90
  42.9 6.2 %collective-permute-start.2 = (bf16[1024,256]{1,0:T(8,128)(2,1)}, bf16[1024,256]{1,0:T(8,128)(2,1)S(1)}, u32[]{:S(2)}, u32[]{:S(2)}) collective-permute-start(bf16[1024,256]{1,0:T(8,128)(2,1)} %refs_0_.1), channel_id=1, source_target_pairs={{0,1},{1,2},{2,3},{3,4},{4,5},{5,6},{6,7},{7,8},{8,9},{9,10},{10,1... | collective-permute-start | bytes 1572872 | tf_op jit(solution)/shard_map/ppermute | solution.py:97
  49.1 3.4 %collective-permute-start.3 = (bf16[1024,256]{1,0:T(8,128)(2,1)}, bf16[1024,256]{1,0:T(8,128)(2,1)S(1)}, u32[]{:S(2)}, u32[]{:S(2)}) collective-permute-start(bf16[1024,256]{1,0:T(8,128)(2,1)} %refs_0_.1), channel_id=1, source_target_pairs={{0,15},{1,0},{2,1},{3,2},{4,3},{5,4},{6,5},{7,6},{8,7},{9,8},{10,9... | collective-permute-start | bytes 1572872 | tf_op jit(solution)/shard_map/ppermute | solution.py:98
  52.5 7.9 %collective-permute-done.2.refs_1_ = bf16[1024,256]{1,0:T(8,128)(2,1)S(1)} collective-permute-done((bf16[1024,256]{1,0:T(8,128)(2,1)}, bf16[1024,256]{1,0:T(8,128)(2,1)S(1)}, u32[]{:S(2)}, u32[]{:S(2)}) %collective-permute-start.2) | collective-permute-done | bytes 524320 | tf_op jit(solution)/shard_map/ppermute | solution.py:97
  60.5 3.9 %collective-permute-start.4 = (bf16[1024,256]{1,0:T(8,128)(2,1)S(1)}, bf16[1024,256]{1,0:T(8,128)(2,1)S(1)}, u32[]{:S(2)}, u32[]{:S(2)}) collective-permute-start(bf16[1024,256]{1,0:T(8,128)(2,1)S(1)} %collective-permute-done.2.refs_1_), channel_id=1, source_target_pairs={{0,1},{1,2},{2,3},{3,4},{4,5},{5,6},{6,7},{7,8},{8,9},{9,10},{10,1... | collective-permute-start | bytes 1572872 | tf_op jit(solution)/shard_map/ppermute | solution.py:97
  64.4 3.1 %collective-permute-start.5 = (bf16[1024,256]{1,0:T(8,128)(2,1)S(1)}, bf16[1024,256]{1,0:T(8,128)(2,1)S(1)}, u32[]{:S(2)}, u32[]{:S(2)}) collective-permute-start(bf16[1024,256]{1,0:T(8,128)(2,1)S(1)} %collective-permute-done.3.refs_2_), channel_id=1, source_target_pairs={{0,15},{1,0},{2,1},{3,2},{4,3},{5,4},{6,5},{7,6},{8,7},{9,8},{10,9... | collective-permute-start | bytes 1572872 | tf_op jit(solution)/shard_map/ppermute | solution.py:98
  68.3 8.0 %collective-permute-done.4.refs_3_ = bf16[1024,256]{1,0:T(8,128)(2,1)S(1)} collective-permute-done((bf16[1024,256]{1,0:T(8,128)(2,1)S(1)}, bf16[1024,256]{1,0:T(8,128)(2,1)S(1)}, u32[]{:S(2)}, u32[]{:S(2)}) %collective-permute-start.4) | collective-permute-done | bytes 524320 | tf_op jit(solution)/shard_map/ppermute | solution.py:97
  76.3 6.6 %collective-permute-start.6 = (bf16[1024,256]{1,0:T(8,128)(2,1)S(1)}, bf16[1024,256]{1,0:T(8,128)(2,1)S(1)}, u32[]{:S(2)}, u32[]{:S(2)}) collective-permute-start(bf16[1024,256]{1,0:T(8,128)(2,1)S(1)} %collective-permute-done.4.refs_3_), channel_id=1, source_target_pairs={{0,1},{1,2},{2,3},{3,4},{4,5},{5,6},{6,7},{7,8},{8,9},{9,10},{10,1... | collective-permute-start | bytes 1572872 | tf_op jit(solution)/shard_map/ppermute | solution.py:97
  87.0 6.6 %collective-permute-done.6.refs_5_ = bf16[1024,256]{1,0:T(8,128)(2,1)S(1)} collective-permute-done((bf16[1024,256]{1,0:T(8,128)(2,1)S(1)}, bf16[1024,256]{1,0:T(8,128)(2,1)S(1)}, u32[]{:S(2)}, u32[]{:S(2)}) %collective-permute-start.6) | collective-permute-done | bytes 524320 | tf_op jit(solution)/shard_map/ppermute | solution.py:97
  93.6 4.6 %collective-permute-start.8 = (bf16[1024,256]{1,0:T(8,128)(2,1)S(1)}, bf16[1024,256]{1,0:T(8,128)(2,1)S(1)}, u32[]{:S(2)}, u32[]{:S(2)}) collective-permute-start(bf16[1024,256]{1,0:T(8,128)(2,1)S(1)} %collective-permute-done.6.refs_5_), channel_id=1, source_target_pairs={{0,1},{1,2},{2,3},{3,4},{4,5},{5,6},{6,7},{7,8},{8,9},{9,10},{10,1... | collective-permute-start | bytes 1572872 | tf_op jit(solution)/shard_map/ppermute | solution.py:97
  100.8 2.5 %collective-permute-start.9 = (bf16[1024,256]{1,0:T(8,128)(2,1)S(1)}, bf16[1024,256]{1,0:T(8,128)(2,1)S(1)}, u32[]{:S(2)}, u32[]{:S(2)}) collective-permute-start(bf16[1024,256]{1,0:T(8,128)(2,1)S(1)} %collective-permute-done.7.refs_6_), channel_id=1, source_target_pairs={{0,15},{1,0},{2,1},{3,2},{4,3},{5,4},{6,5},{7,6},{8,7},{9,8},{10,9... | collective-permute-start | bytes 1572872 | tf_op jit(solution)/shard_map/ppermute | solution.py:98
  104.1 7.3 %collective-permute-done.8.refs_7_ = bf16[1024,256]{1,0:T(8,128)(2,1)S(1)} collective-permute-done((bf16[1024,256]{1,0:T(8,128)(2,1)S(1)}, bf16[1024,256]{1,0:T(8,128)(2,1)S(1)}, u32[]{:S(2)}, u32[]{:S(2)}) %collective-permute-start.8) | collective-permute-done | bytes 524320 | tf_op jit(solution)/shard_map/ppermute | solution.py:97
  114.1 2.2 collective-permute-done.9.refs_8_
  116.3 3.4 %collective-permute-start.11 = (bf16[1024,256]{1,0:T(8,128)(2,1)S(1)}, bf16[1024,256]{1,0:T(8,128)(2,1)S(1)}, u32[]{:S(2)}, u32[]{:S(2)}) collective-permute-start(bf16[1024,256]{1,0:T(8,128)(2,1)S(1)} %collective-permute-done.9.refs_8_), channel_id=1, source_target_pairs={{0,15},{1,0},{2,1},{3,2},{4,3},{5,4},{6,5},{7,6},{8,7},{9,8},{10,9... | collective-permute-start | bytes 1572872 | tf_op jit(solution)/shard_map/ppermute | solution.py:98
  120.6 7.7 %collective-permute-done.10.refs_9_ = bf16[1024,256]{1,0:T(8,128)(2,1)S(1)} collective-permute-done((bf16[1024,256]{1,0:T(8,128)(2,1)S(1)}, bf16[1024,256]{1,0:T(8,128)(2,1)S(1)}, u32[]{:S(2)}, u32[]{:S(2)}) %collective-permute-start.10) | collective-permute-done | bytes 524320 | tf_op jit(solution)/shard_map/ppermute | solution.py:97
  131.1 5.1 %collective-permute-start.13 = (bf16[1024,256]{1,0:T(8,128)(2,1)S(1)}, bf16[1024,256]{1,0:T(8,128)(2,1)S(1)}, u32[]{:S(2)}, u32[]{:S(2)}) collective-permute-start(bf16[1024,256]{1,0:T(8,128)(2,1)S(1)} %collective-permute-done.11.refs_10_), channel_id=1, source_target_pairs={{0,15},{1,0},{2,1},{3,2},{4,3},{5,4},{6,5},{7,6},{8,7},{9,8},{10,9... | collective-permute-start | bytes 1572872 | tf_op jit(solution)/shard_map/ppermute | solution.py:98
  137.0 7.3 %collective-permute-done.12.refs_11_ = bf16[1024,256]{1,0:T(8,128)(2,1)S(1)} collective-permute-done((bf16[1024,256]{1,0:T(8,128)(2,1)S(1)}, bf16[1024,256]{1,0:T(8,128)(2,1)S(1)}, u32[]{:S(2)}, u32[]{:S(2)}) %collective-permute-start.12) | collective-permute-done | bytes 524320 | tf_op jit(solution)/shard_map/ppermute | solution.py:97
  147.1 3.1 %collective-permute-done.13.refs_12_ = bf16[1024,256]{1,0:T(8,128)(2,1)S(1)} collective-permute-done((bf16[1024,256]{1,0:T(8,128)(2,1)S(1)}, bf16[1024,256]{1,0:T(8,128)(2,1)S(1)}, u32[]{:S(2)}, u32[]{:S(2)}) %collective-permute-start.13) | collective-permute-done | bytes 524320 | tf_op jit(solution)/shard_map/ppermute | solution.py:98
  150.2 2.0 collective-permute-start.15
  152.2 4.5 %collective-permute-done.14.refs_0_ = bf16[1024,256]{1,0:T(8,128)(2,1)S(1)} collective-permute-done((bf16[1024,256]{1,0:T(8,128)(2,1)S(1)}, bf16[1024,256]{1,0:T(8,128)(2,1)S(1)}, u32[]{:S(2)}, u32[]{:S(2)}) %collective-permute-start.14) | collective-permute-done | bytes 524320 | tf_op jit(solution)/shard_map/ppermute | solution.py:97
  156.8 1.9 collective-permute-start.16
  158.7 5.8 %collective-permute-done.15.refs_1_ = bf16[1024,256]{1,0:T(8,128)(2,1)S(1)} collective-permute-done((bf16[1024,256]{1,0:T(8,128)(2,1)S(1)}, bf16[1024,256]{1,0:T(8,128)(2,1)S(1)}, u32[]{:S(2)}, u32[]{:S(2)}) %collective-permute-start.15) | collective-permute-done | bytes 524320 | tf_op jit(solution)/shard_map/ppermute | solution.py:98
  165.3 2.2 collective-permute-start.17
  167.5 6.9 %collective-permute-done.17 = bf16[512,256]{1,0:T(8,128)(2,1)} collective-permute-done((bf16[512,256]{1,0:T(8,128)(2,1)S(1)}, bf16[512,256]{1,0:T(8,128)(2,1)}, u32[]{:S(2)}, u32[]{:S(2)}) %collective-permute-start.17) | collective-permute-done | bytes 262176 | tf_op jit(solution)/shard_map/ppermute | solution.py:103
  175.5 2.2 copy-done
  189.2 4.4 %shard_map.68.base_ref = f32[1024,512]{1,0:T(8,128)S(1)} custom-call(s32[1]{0:T(128)} %bitcast.z_ref, bf16[1024,512]{1,0:T(8,128)(2,1)S(1)} %copy-done.4, bf16[8,4,64,1024]{3,2,1,0:T(8,128)(2,1)S(1)} %bitcast.3, bf16[1024,256]{1,0:T(8,128)(2,1)S(1)} %copy-done.5, bf16[1024,256]{1,0:T(8,128)(2,1)S(1)} %collective-permute-done.2.refs_1_, ...), custom_call_target="tpu_custom_call" | custom-call | flops 3489660928 | bytes 15204352 | tf_op jit(solution)/shard_map/pallas_call | solution.py:67
  193.6 4.8 %shard_map.69 = (f32[1024,512]{1,0:T(8,128)S(1)}, f32[8,1024]{1,0:T(8,128)S(1)}) custom-call(s32[1]{0:T(128)} %bitcast.z_ref, f32[1024,512]{1,0:T(8,128)S(1)} %shard_map.68.base_ref, bf16[8,4,64,1024]{3,2,1,0:T(8,128)(2,1)S(1)} %bitcast.4, bf16[1024,256]{1,0:T(8,128)(2,1)S(1)} %collective-permute-done.14.refs_0_, bf16[1024,256]{1,0:T(8,128)(2,1)S(1)} %copy-done.3, ...), custom_call_target="tpu_custom_call" | custom-call | flops 805306368 | bytes 9961472 | tf_op jit(solution)/shard_map/pallas_call | solution.py:67
  199.1 9.0 %all-to-all-start = ((f32[16,1,1024]{2,1,0:T(1,128)}), f32[16,1,1024]{2,1,0:T(1,128)S(1)}, u32[]{:S(2)}, u32[]{:S(2)}) async-start(f32[16,1,1024]{2,1,0:T(1,128)} %broadcast_in_dim.2), calls=%async_computation | async-start | bytes 131072 | tf_op jit(solution)/shard_map/all_to_all | solution.py:110
  208.2 12.8 %all-to-all-done = f32[16,1,1024]{2,1,0:T(1,128)S(1)} async-done(((f32[16,1,1024]{2,1,0:T(1,128)}), f32[16,1,1024]{2,1,0:T(1,128)S(1)}, u32[]{:S(2)}, u32[]{:S(2)}) %all-to-all-start) | async-done | bytes 65568 | tf_op jit(solution)/shard_map/all_to_all | solution.py:110
  (81 shorter events, 35.8 us)
Async XLA Ops:
  7.2 168.3 %copy-start.5 = (bf16[1024,256]{1,0:T(8,128)(2,1)S(1)}, bf16[1024,256]{1,0:T(8,128)(2,1)}, u32[]{:S(2)}) copy-start(bf16[1024,256]{1,0:T(8,128)(2,1)} %refs_0_.1) | copy-start | bytes 1572868
  7.2 168.3 %copy-start.4 = (bf16[1024,512]{1,0:T(8,128)(2,1)S(1)}, bf16[1024,512]{1,0:T(8,128)(2,1)}, u32[]{:S(2)}) copy-start(bf16[1024,512]{1,0:T(8,128)(2,1)} %base_ref.1) | copy-start | bytes 3145732
  7.2 168.3 %all-gather.3.cloned.1.call-start = ((), (), s32[]{:S(2)}) async-start(), calls=%async_computation.1 | async-start | bytes 4325376 | tf_op jit(solution)/shard_map/all_gather | solution.py:91
  9.1 10.2 %collective-permute-start = (bf16[64,1024]{1,0:T(8,128)(2,1)S(1)}, bf16[64,1024]{1,0:T(8,128)(2,1)S(1)}, u32[]{:S(2)}, u32[]{:S(2)}) collective-permute-start(bf16[64,1024]{1,0:T(8,128)(2,1)S(1)} %get-tuple-element.6), channel_id=1, source_target_pairs={{0,0},{4,52},{8,40},{12,28},{16,64},{20,116},{24,104},{28,92},{32,... | collective-permute-start | bytes 393224 | tf_op jit(solution)/shard_map/ppermute | solution.py:89
  19.2 23.0 %collective-permute-start.1 = (bf16[64,1024]{1,0:T(8,128)(2,1)S(1)}, bf16[64,1024]{1,0:T(8,128)(2,1)S(1)}, u32[]{:S(2)}, u32[]{:S(2)}) collective-permute-start(bf16[64,1024]{1,0:T(8,128)(2,1)S(1)} %collective-permute-done), channel_id=1, source_target_pairs={{0,0},{52,48},{40,32},{28,16},{64,64},{116,112},{104,96},{92,80},{... | collective-permute-start | bytes 393224 | tf_op jit(solution)/shard_map/ppermute | solution.py:90
  42.9 17.6 %collective-permute-start.2 = (bf16[1024,256]{1,0:T(8,128)(2,1)}, bf16[1024,256]{1,0:T(8,128)(2,1)S(1)}, u32[]{:S(2)}, u32[]{:S(2)}) collective-permute-start(bf16[1024,256]{1,0:T(8,128)(2,1)} %refs_0_.1), channel_id=1, source_target_pairs={{0,1},{1,2},{2,3},{3,4},{4,5},{5,6},{6,7},{7,8},{8,9},{9,10},{10,1... | collective-permute-start | bytes 1572872 | tf_op jit(solution)/shard_map/ppermute | solution.py:97
  49.1 15.3 %collective-permute-start.3 = (bf16[1024,256]{1,0:T(8,128)(2,1)}, bf16[1024,256]{1,0:T(8,128)(2,1)S(1)}, u32[]{:S(2)}, u32[]{:S(2)}) collective-permute-start(bf16[1024,256]{1,0:T(8,128)(2,1)} %refs_0_.1), channel_id=1, source_target_pairs={{0,15},{1,0},{2,1},{3,2},{4,3},{5,4},{6,5},{7,6},{8,7},{9,8},{10,9... | collective-permute-start | bytes 1572872 | tf_op jit(solution)/shard_map/ppermute | solution.py:98
  60.5 15.9 %collective-permute-start.4 = (bf16[1024,256]{1,0:T(8,128)(2,1)S(1)}, bf16[1024,256]{1,0:T(8,128)(2,1)S(1)}, u32[]{:S(2)}, u32[]{:S(2)}) collective-permute-start(bf16[1024,256]{1,0:T(8,128)(2,1)S(1)} %collective-permute-done.2.refs_1_), channel_id=1, source_target_pairs={{0,1},{1,2},{2,3},{3,4},{4,5},{5,6},{6,7},{7,8},{8,9},{9,10},{10,1... | collective-permute-start | bytes 1572872 | tf_op jit(solution)/shard_map/ppermute | solution.py:97
  64.4 19.9 %collective-permute-start.5 = (bf16[1024,256]{1,0:T(8,128)(2,1)S(1)}, bf16[1024,256]{1,0:T(8,128)(2,1)S(1)}, u32[]{:S(2)}, u32[]{:S(2)}) collective-permute-start(bf16[1024,256]{1,0:T(8,128)(2,1)S(1)} %collective-permute-done.3.refs_2_), channel_id=1, source_target_pairs={{0,15},{1,0},{2,1},{3,2},{4,3},{5,4},{6,5},{7,6},{8,7},{9,8},{10,9... | collective-permute-start | bytes 1572872 | tf_op jit(solution)/shard_map/ppermute | solution.py:98
  76.3 17.3 %collective-permute-start.6 = (bf16[1024,256]{1,0:T(8,128)(2,1)S(1)}, bf16[1024,256]{1,0:T(8,128)(2,1)S(1)}, u32[]{:S(2)}, u32[]{:S(2)}) collective-permute-start(bf16[1024,256]{1,0:T(8,128)(2,1)S(1)} %collective-permute-done.4.refs_3_), channel_id=1, source_target_pairs={{0,1},{1,2},{2,3},{3,4},{4,5},{5,6},{6,7},{7,8},{8,9},{9,10},{10,1... | collective-permute-start | bytes 1572872 | tf_op jit(solution)/shard_map/ppermute | solution.py:97
  84.3 16.5 %collective-permute-start.7 = (bf16[1024,256]{1,0:T(8,128)(2,1)S(1)}, bf16[1024,256]{1,0:T(8,128)(2,1)S(1)}, u32[]{:S(2)}, u32[]{:S(2)}) collective-permute-start(bf16[1024,256]{1,0:T(8,128)(2,1)S(1)} %collective-permute-done.5.refs_4_), channel_id=1, source_target_pairs={{0,15},{1,0},{2,1},{3,2},{4,3},{5,4},{6,5},{7,6},{8,7},{9,8},{10,9... | collective-permute-start | bytes 1572872 | tf_op jit(solution)/shard_map/ppermute | solution.py:98
  93.6 17.8 %collective-permute-start.8 = (bf16[1024,256]{1,0:T(8,128)(2,1)S(1)}, bf16[1024,256]{1,0:T(8,128)(2,1)S(1)}, u32[]{:S(2)}, u32[]{:S(2)}) collective-permute-start(bf16[1024,256]{1,0:T(8,128)(2,1)S(1)} %collective-permute-done.6.refs_5_), channel_id=1, source_target_pairs={{0,1},{1,2},{2,3},{3,4},{4,5},{5,6},{6,7},{7,8},{8,9},{9,10},{10,1... | collective-permute-start | bytes 1572872 | tf_op jit(solution)/shard_map/ppermute | solution.py:97
  100.8 15.5 %collective-permute-start.9 = (bf16[1024,256]{1,0:T(8,128)(2,1)S(1)}, bf16[1024,256]{1,0:T(8,128)(2,1)S(1)}, u32[]{:S(2)}, u32[]{:S(2)}) collective-permute-start(bf16[1024,256]{1,0:T(8,128)(2,1)S(1)} %collective-permute-done.7.refs_6_), channel_id=1, source_target_pairs={{0,15},{1,0},{2,1},{3,2},{4,3},{5,4},{6,5},{7,6},{8,7},{9,8},{10,9... | collective-permute-start | bytes 1572872 | tf_op jit(solution)/shard_map/ppermute | solution.py:98
  111.4 16.9 %collective-permute-start.10 = (bf16[1024,256]{1,0:T(8,128)(2,1)S(1)}, bf16[1024,256]{1,0:T(8,128)(2,1)S(1)}, u32[]{:S(2)}, u32[]{:S(2)}) collective-permute-start(bf16[1024,256]{1,0:T(8,128)(2,1)S(1)} %collective-permute-done.8.refs_7_), channel_id=1, source_target_pairs={{0,1},{1,2},{2,3},{3,4},{4,5},{5,6},{6,7},{7,8},{8,9},{9,10},{10,1... | collective-permute-start | bytes 1572872 | tf_op jit(solution)/shard_map/ppermute | solution.py:97
  116.3 14.8 %collective-permute-start.11 = (bf16[1024,256]{1,0:T(8,128)(2,1)S(1)}, bf16[1024,256]{1,0:T(8,128)(2,1)S(1)}, u32[]{:S(2)}, u32[]{:S(2)}) collective-permute-start(bf16[1024,256]{1,0:T(8,128)(2,1)S(1)} %collective-permute-done.9.refs_8_), channel_id=1, source_target_pairs={{0,15},{1,0},{2,1},{3,2},{4,3},{5,4},{6,5},{7,6},{8,7},{9,8},{10,9... | collective-permute-start | bytes 1572872 | tf_op jit(solution)/shard_map/ppermute | solution.py:98
  128.3 16.1 %collective-permute-start.12 = (bf16[1024,256]{1,0:T(8,128)(2,1)S(1)}, bf16[1024,256]{1,0:T(8,128)(2,1)S(1)}, u32[]{:S(2)}, u32[]{:S(2)}) collective-permute-start(bf16[1024,256]{1,0:T(8,128)(2,1)S(1)} %collective-permute-done.10.refs_9_), channel_id=1, source_target_pairs={{0,1},{1,2},{2,3},{3,4},{4,5},{5,6},{6,7},{7,8},{8,9},{9,10},{10,1... | collective-permute-start | bytes 1572872 | tf_op jit(solution)/shard_map/ppermute | solution.py:97
  131.1 19.1 %collective-permute-start.13 = (bf16[1024,256]{1,0:T(8,128)(2,1)S(1)}, bf16[1024,256]{1,0:T(8,128)(2,1)S(1)}, u32[]{:S(2)}, u32[]{:S(2)}) collective-permute-start(bf16[1024,256]{1,0:T(8,128)(2,1)S(1)} %collective-permute-done.11.refs_10_), channel_id=1, source_target_pairs={{0,15},{1,0},{2,1},{3,2},{4,3},{5,4},{6,5},{7,6},{8,7},{9,8},{10,9... | collective-permute-start | bytes 1572872 | tf_op jit(solution)/shard_map/ppermute | solution.py:98
  144.4 12.4 %collective-permute-start.14 = (bf16[1024,256]{1,0:T(8,128)(2,1)S(1)}, bf16[1024,256]{1,0:T(8,128)(2,1)S(1)}, u32[]{:S(2)}, u32[]{:S(2)}) collective-permute-start(bf16[1024,256]{1,0:T(8,128)(2,1)S(1)} %collective-permute-done.12.refs_11_), channel_id=1, source_target_pairs={{0,1},{1,2},{2,3},{3,4},{4,5},{5,6},{6,7},{7,8},{8,9},{9,10},{10,1... | collective-permute-start | bytes 1572872 | tf_op jit(solution)/shard_map/ppermute | solution.py:97
  150.2 14.3 %copy-start.26 = (bf16[1024,256]{1,0:T(8,128)(2,1)}, bf16[1024,256]{1,0:T(8,128)(2,1)S(1)}, u32[]{:S(2)}) copy-start(bf16[1024,256]{1,0:T(8,128)(2,1)S(1)} %collective-permute-done.13.refs_12_) | copy-start | bytes 1572868
  150.2 14.3 %collective-permute-start.15 = (bf16[1024,256]{1,0:T(8,128)(2,1)S(1)}, bf16[1024,256]{1,0:T(8,128)(2,1)S(1)}, u32[]{:S(2)}, u32[]{:S(2)}) collective-permute-start(bf16[1024,256]{1,0:T(8,128)(2,1)S(1)} %collective-permute-done.13.refs_12_), channel_id=1, source_target_pairs={{0,15},{1,0},{2,1},{3,2},{4,3},{5,4},{6,5},{7,6},{8,7},{9,8},{10,9... | collective-permute-start | bytes 1572872 | tf_op jit(solution)/shard_map/ppermute | solution.py:98
  156.8 10.8 %collective-permute-start.16 = (bf16[512,256]{1,0:T(8,128)(2,1)S(1)}, bf16[512,256]{1,0:T(8,128)(2,1)S(1)}, u32[]{:S(2)}, u32[]{:S(2)}) collective-permute-start(bf16[512,256]{1,0:T(8,128)(2,1)S(1)} %slice.15), channel_id=1, source_target_pairs={{0,1},{1,2},{2,3},{3,4},{4,5},{5,6},{6,7},{7,8},{8,9},{9,10},{10,1... | collective-permute-start | bytes 786440 | tf_op jit(solution)/shard_map/ppermute | solution.py:102
  165.3 9.2 %collective-permute-start.17 = (bf16[512,256]{1,0:T(8,128)(2,1)S(1)}, bf16[512,256]{1,0:T(8,128)(2,1)}, u32[]{:S(2)}, u32[]{:S(2)}) collective-permute-start(bf16[512,256]{1,0:T(8,128)(2,1)S(1)} %slice.16), channel_id=1, source_target_pairs={{0,15},{1,0},{2,1},{3,2},{4,3},{5,4},{6,5},{7,6},{8,7},{9,8},{10,9... | collective-permute-start | bytes 786440 | tf_op jit(solution)/shard_map/ppermute | solution.py:103
  175.5 2.2 copy-start
  177.7 1.0 copy-start.7
  178.7 1.0 copy-start.9
  179.8 1.0 copy-start.11
  180.8 1.0 copy-start.13
  181.9 1.0 copy-start.15
  189.2 4.4 %copy-start.1 = (bf16[2048,1024]{1,0:T(8,128)(2,1)S(1)}, bf16[2048,1024]{1,0:T(8,128)(2,1)}, u32[]{:S(2)}) copy-start(bf16[2048,1024]{1,0:T(8,128)(2,1)} %all-gather.3.cloned.1.call-done) | copy-start | bytes 12582916
  189.2 4.4 %copy-start.3 = (bf16[1024,256]{1,0:T(8,128)(2,1)S(1)}, bf16[1024,256]{1,0:T(8,128)(2,1)}, u32[]{:S(2)}) copy-start(bf16[1024,256]{1,0:T(8,128)(2,1)} %copy-done.2) | copy-start | bytes 1572868
  193.6 14.5 %copy-start.29 = (bf16[512]{0:T(512)(128)(2,1)S(1)}, bf16[512]{0:T(512)(128)(2,1)}, u32[]{:S(2)}) copy-start(bf16[512]{0:T(512)(128)(2,1)} %param.9) | copy-start | bytes 3076
  199.1 21.8 %all-to-all-start = ((f32[16,1,1024]{2,1,0:T(1,128)}), f32[16,1,1024]{2,1,0:T(1,128)S(1)}, u32[]{:S(2)}, u32[]{:S(2)}) async-start(f32[16,1,1024]{2,1,0:T(1,128)} %broadcast_in_dim.2), calls=%async_computation | async-start | bytes 131072 | tf_op jit(solution)/shard_map/all_to_all | solution.py:110
  (18 other events, 15.8 us)
Sparse Core Ops, SparseCore 0:
  43.0 62.1 all-gather.2

commit v2 on v0

v2 whole, which is shorter than its diff:
```python
import jax
import jax.numpy as jnp
from jax import lax
from jax.experimental import pallas as pl
from jax.experimental.pallas import tpu as pltpu
from jax.sharding import PartitionSpec as P

D = 8192
H = 4096
Z = ("tx", "ty")
ALL = ("fsdp", "tx", "ty")
NZ = 16

mix_rate = 0.6

TOK = 1024
FEAT = 256
COLS = 512
TILE = 256


def place(f, t, y):
    return (f * 4 + t) * 4 + y


def column(r, turn):
    return ((r % 4) * 4 + (turn % 2) * 2 + r // 4) * 2 + turn // 2


SPREAD = []
for y in range(4):
    for u in range(4):
        for r in range(8):
            for t in range(4):
                SPREAD.append((place(8 * u + r, t, y), place(column(r, (u - t + y) % 4), u, y)))


def partner(dx, dy, dc):
    pairs = []
    for x in range(4):
        for y in range(4):
            for c in range(2):
                pairs.append(((x * 4 + y) * 2 + c, ((x ^ dx) * 4 + (y ^ dy)) * 2 + (c ^ dc)))
    return pairs


def kernel(z_ref, base_ref, weight_ref, context_ref, out_ref, squares_ref):
    part = pl.program_id(0)
    first = z_ref[0] // 4 + z_ref[0] % 4
    block = jnp.concatenate(
        [context_ref[(first - turn + 4) % 4 * 4 + i] for turn in range(4) for i in range(4)],
        axis=1,
    )
    total = base_ref[...].astype(jnp.float32) + jnp.dot(
        block, weight_ref[...], preferred_element_type=jnp.float32
    )
    out_ref[...] = total
    squared = total * total
    lanes = sum(squared[:, i * 128 : (i + 1) * 128] for i in range(COLS // 128))
    sums = jnp.sum(lanes.T, axis=0, keepdims=True)
    for i in range(TILE // 128):
        squares_ref[:, pl.ds(part * (TILE // 128) + i, 1), :] = jnp.broadcast_to(
            sums[:, i * 128 : (i + 1) * 128][None], (NZ, 1, 128)
        )


def product(z, base, weight, context):
    row = lambda i, z: (i, 0)
    return pl.pallas_call(
        kernel,
        out_shape=[
            jax.ShapeDtypeStruct((TOK, COLS), jnp.float32),
            jax.ShapeDtypeStruct((NZ, TOK // 128, 128), jnp.float32),
        ],
        grid_spec=pltpu.PrefetchScalarGridSpec(
            num_scalar_prefetch=1,
            grid=(TOK // TILE,),
            in_specs=[
                pl.BlockSpec((TILE, COLS), row),
                pl.BlockSpec((H, COLS), lambda i, z: (0, 0)),
                pl.BlockSpec((NZ, TILE, FEAT), lambda i, z: (0, i, 0)),
            ],
            out_specs=[
                pl.BlockSpec((TILE, COLS), row),
                pl.BlockSpec((NZ, TOK // 128, 128), lambda i, z: (0, 0, 0)),
            ],
        ),
        compiler_params=pltpu.CompilerParams(vmem_limit_bytes=58 * 1024 * 1024),
        cost_estimate=pl.CostEstimate(
            flops=2 * TOK * COLS * H,
            bytes_accessed=(TOK + COLS) * H * 2 + TOK * COLS * 6,
            transcendentals=0,
        ),
    )(z, base, weight, context)


def shards(context, residual, policy_weight, master_weight, norm_gain):
    new_master = mix_rate * policy_weight.astype(jnp.float32) + (1.0 - mix_rate) * master_weight
    recast = new_master.astype(jnp.bfloat16)

    z = (lax.axis_index("tx") * 4 + lax.axis_index("ty")).astype(jnp.int32)
    f = lax.axis_index("fsdp")
    x, y, c = f // 8, (f // 2) % 4, f % 2

    gathered = lax.all_gather(context, Z, axis=0)
    piece = lax.ppermute(recast, ALL, SPREAD)

    row = jnp.zeros((4, 64, 1024), jnp.bfloat16)
    for dx in range(4):
        got = piece if dx == 0 else lax.ppermute(piece, "fsdp", partner(dx, 0, 0))
        row = lax.dynamic_update_slice(row, got[None], (x ^ dx, 0, 0))
    near = lax.ppermute(row, "fsdp", partner(0, 1, 0))
    back = lax.ppermute(row, "fsdp", partner(0, 3, 0))
    low = lax.ppermute(back[:2], "fsdp", partner(0, 1, 0))
    high = lax.ppermute(near[2:], "fsdp", partner(0, 3, 0))
    plane = jnp.zeros((16, 64, 1024), jnp.bfloat16)
    for got, dy, at in ((row, 0, 0), (near, 1, 0), (back, 3, 0), (low, 2, 0), (high, 2, 2)):
        plane = lax.dynamic_update_slice(plane, got, ((y ^ dy) * 4 + at, 0, 0))
    other = lax.ppermute(plane, "fsdp", partner(0, 0, 1))
    pieces = jnp.zeros((32, 64, 1024), jnp.bfloat16)
    pieces = lax.dynamic_update_slice(pieces, plane, (c * 16, 0, 0))
    pieces = lax.dynamic_update_slice(pieces, other, ((1 - c) * 16, 0, 0))
    weight = pieces.reshape(4, COLS, 1024).transpose(0, 2, 1).reshape(H, COLS)
    hidden, squares = product(z[None], residual, weight, gathered)

    totals = jnp.sum(lax.all_to_all(squares, Z, 0, 0, tiled=True), axis=0)
    square_mean = (totals.reshape(TOK) / D)[:, None]
    normed = (
        hidden * lax.rsqrt(square_mean + 1e-05) * norm_gain.astype(jnp.float32)[None, :]
    ).astype(jnp.bfloat16)
    return (normed, new_master)


def solution(mesh):
    return jax.shard_map(
        shards,
        mesh=mesh,
        in_specs=(
            P("fsdp", ("tx", "ty")),
            P("fsdp", ("ty", "tx")),
            P(("ty", "fsdp"), "tx"),
            P(("ty", "fsdp"), "tx"),
            P(("ty", "tx")),
        ),
        out_specs=(P("fsdp", ("ty", "tx")), P(("ty", "fsdp"), "tx")),
        check_vma=False,
    )
```

time: 410 us -> 168 us (0.41)
  the two profiles are of different devices: /device:TPU:6 before, /device:TPU:12 now
where the time goes in v2:
time: 168 us; the launch traced here: 167 us
  starting transfers between devices  65.9 us (39%)
  waiting for transfers between devices  56.7 us (34%)
  local copies, waits for them, and re-layouts  16 us (10%)
  between operations  14.3 us (9%)
  Pallas kernels  9.56 us (6%)
  other arithmetic  4.57 us (3%)
    ppermute x3, starting transfers between devices, shards(): got = piece if dx == 0 else lax.ppermute(piece, 'fsdp', partner(dx, 0, 0))  22.7 us
    all_gather x1, waiting for transfers between devices, shards(): gathered = lax.all_gather(context, Z, axis=0)  16.9 us
    ppermute x1, starting transfers between devices, shards(): piece = lax.ppermute(recast, ALL, SPREAD)  15 us
    all_to_all x1, starting transfers between devices, shards(): totals = jnp.sum(lax.all_to_all(squares, Z, 0, 0, tiled=True), axis=0)  14.4 us
    all_to_all x1, waiting for transfers between devices, shards(): totals = jnp.sum(lax.all_to_all(squares, Z, 0, 0, tiled=True), axis=0)  13 us
    ppermute x1, waiting for transfers between devices, shards(): back = lax.ppermute(row, 'fsdp', partner(0, 3, 0))  10.3 us
    pallas_call x1, Pallas kernels, product(): pl.pallas_call(kernel, out_shape=[jax.ShapeDtypeStruct((TOK, COLS), jnp.f...  9.56 us
    transpose x1, local copies, waits for them, and re-layouts, shards(): weight = pieces.reshape(4, COLS, 1024).transpose(0, 2, 1).reshape(H, COLS)  6.25 us
  transfers between devices with their start and end apart: 11, of which 9 were waited for; matrix products, arithmetic and copies ran while one was open for 11% of the time, Pallas kernels for 0%

profile of v2, /device:TPU:12, one launch (start us, length us, event | category | flops | bytes accessed | tf_op | source)
XLA Modules:
  0.0 167.1 jit_solution(621761326715191844)
XLA Ops:
  7.2 0.0 all-gather.3.cloned.1.call-start
  7.2 0.7 all-gather.3.cloned.1.call-update
  7.9 1.7 %fusion = (bf16[64,1024]{1,0:T(8,128)(2,1)S(1)}, f32[64,1024]{1,0:T(8,128)}) fusion(f32[64,1024]{1,0:T(8,128)} %param.8, bf16[64,1024]{1,0:T(8,128)(2,1)} %param.7), kind=kLoop, calls=%fused_computation.14 | loop fusion | flops 327680 | bytes 786432 | tf_op jit(solution)/shard_map/convert_element_type | solution.py:99
  9.6 15.0 %collective-permute-start = (bf16[64,1024]{1,0:T(8,128)(2,1)S(1)}, bf16[64,1024]{1,0:T(8,128)(2,1)S(1)}, u32[]{:S(2)}, u32[]{:S(2)}) collective-permute-start(bf16[64,1024]{1,0:T(8,128)(2,1)S(1)} %get-tuple-element.6), channel_id=1, source_target_pairs={{0,0},{4,80},{8,16},{12,64},{16,128},{20,208},{24,144},{28,192},{3... | collective-permute-start | bytes 393224 | tf_op jit(solution)/shard_map/ppermute | solution.py:106
  24.7 3.8 %collective-permute-done = bf16[64,1024]{1,0:T(8,128)(2,1)S(1)} collective-permute-done((bf16[64,1024]{1,0:T(8,128)(2,1)S(1)}, bf16[64,1024]{1,0:T(8,128)(2,1)S(1)}, u32[]{:S(2)}, u32[]{:S(2)}) %collective-permute-start) | collective-permute-done | bytes 131104 | tf_op jit(solution)/shard_map/ppermute | solution.py:106
  28.5 17.4 %collective-permute-start.1 = (bf16[64,1024]{1,0:T(8,128)(2,1)S(1)}, bf16[64,1024]{1,0:T(8,128)(2,1)S(1)}, u32[]{:S(2)}, u32[]{:S(2)}) collective-permute-start(bf16[64,1024]{1,0:T(8,128)(2,1)S(1)} %collective-permute-done), channel_id=1, source_target_pairs={{0,128},{16,144},{32,160},{48,176},{64,192},{80,208},{96,224},{112... | collective-permute-start | bytes 393224 | tf_op jit(solution)/shard_map/ppermute | solution.py:110
  45.9 1.9 %collective-permute-start.2 = (bf16[64,1024]{1,0:T(8,128)(2,1)S(1)}, bf16[64,1024]{1,0:T(8,128)(2,1)S(1)}, u32[]{:S(2)}, u32[]{:S(2)}) collective-permute-start(bf16[64,1024]{1,0:T(8,128)(2,1)S(1)} %collective-permute-done), channel_id=1, source_target_pairs={{0,256},{16,272},{32,288},{48,304},{64,320},{80,336},{96,352},{112... | collective-permute-start | bytes 393224 | tf_op jit(solution)/shard_map/ppermute | solution.py:110
  47.9 3.4 %collective-permute-start.3 = (bf16[64,1024]{1,0:T(8,128)(2,1)S(1)}, bf16[64,1024]{1,0:T(8,128)(2,1)S(1)}, u32[]{:S(2)}, u32[]{:S(2)}) collective-permute-start(bf16[64,1024]{1,0:T(8,128)(2,1)S(1)} %collective-permute-done), channel_id=1, source_target_pairs={{0,384},{16,400},{32,416},{48,432},{64,448},{80,464},{96,480},{112... | collective-permute-start | bytes 393224 | tf_op jit(solution)/shard_map/ppermute | solution.py:110
  51.2 0.1 broadcast_in_dim.29
  51.4 3.1 %collective-permute-done.2 = bf16[64,1024]{1,0:T(8,128)(2,1)S(1)} collective-permute-done((bf16[64,1024]{1,0:T(8,128)(2,1)S(1)}, bf16[64,1024]{1,0:T(8,128)(2,1)S(1)}, u32[]{:S(2)}, u32[]{:S(2)}) %collective-permute-start.2) | collective-permute-done | bytes 131104 | tf_op jit(solution)/shard_map/ppermute | solution.py:110
  54.4 2.7 %collective-permute-done.3 = bf16[64,1024]{1,0:T(8,128)(2,1)S(1)} collective-permute-done((bf16[64,1024]{1,0:T(8,128)(2,1)S(1)}, bf16[64,1024]{1,0:T(8,128)(2,1)S(1)}, u32[]{:S(2)}, u32[]{:S(2)}) %collective-permute-start.3) | collective-permute-done | bytes 131104 | tf_op jit(solution)/shard_map/ppermute | solution.py:110
  57.2 4.0 %collective-permute-start.5 = (bf16[4,64,1024]{2,1,0:T(8,128)(2,1)S(1)}, bf16[4,64,1024]{2,1,0:T(8,128)(2,1)S(1)}, u32[]{:S(2)}, u32[]{:S(2)}) collective-permute-start(bf16[4,64,1024]{2,1,0:T(8,128)(2,1)S(1)} %bitcast_dynamic-update-slice_fusion), channel_id=1, source_target_pairs={{0,96},{16,112},{32,64},{48,80},{64,32},{80,48},{96,0},{112,16},{1... | collective-permute-start | bytes 1572872 | tf_op jit(solution)/shard_map/ppermute | solution.py:113
  61.2 1.9 %collective-permute-start.4 = (bf16[4,64,1024]{2,1,0:T(8,128)(2,1)S(1)}, bf16[4,64,1024]{2,1,0:T(8,128)(2,1)}, u32[]{:S(2)}, u32[]{:S(2)}) collective-permute-start(bf16[4,64,1024]{2,1,0:T(8,128)(2,1)S(1)} %bitcast_dynamic-update-slice_fusion), channel_id=1, source_target_pairs={{0,32},{16,48},{32,0},{48,16},{64,96},{80,112},{96,64},{112,80},{1... | collective-permute-start | bytes 1572872 | tf_op jit(solution)/shard_map/ppermute | solution.py:112
  63.2 10.3 %collective-permute-done.5 = bf16[4,64,1024]{2,1,0:T(8,128)(2,1)S(1)} collective-permute-done((bf16[4,64,1024]{2,1,0:T(8,128)(2,1)S(1)}, bf16[4,64,1024]{2,1,0:T(8,128)(2,1)S(1)}, u32[]{:S(2)}, u32[]{:S(2)}) %collective-permute-start.5) | collective-permute-done | bytes 524320 | tf_op jit(solution)/shard_map/ppermute | solution.py:113
  73.5 3.9 %collective-permute-start.6 = (bf16[2,64,1024]{2,1,0:T(8,128)(2,1)S(1)}, bf16[2,64,1024]{2,1,0:T(8,128)(2,1)S(1)}, u32[]{:S(2)}, u32[]{:S(2)}) collective-permute-start(bf16[2,64,1024]{2,1,0:T(8,128)(2,1)S(1)} %slice.8), channel_id=1, source_target_pairs={{0,32},{16,48},{32,0},{48,16},{64,96},{80,112},{96,64},{112,80},{1... | collective-permute-start | bytes 786440 | tf_op jit(solution)/shard_map/ppermute | solution.py:114
  77.4 0.3 broadcast_in_dim.28
  77.7 1.0 slice.9
  78.7 1.9 %collective-permute-start.7 = (bf16[2,64,1024]{2,1,0:T(8,128)(2,1)S(1)}, bf16[2,64,1024]{2,1,0:T(8,128)(2,1)S(1)}, u32[]{:S(2)}, u32[]{:S(2)}) collective-permute-start(bf16[2,64,1024]{2,1,0:T(8,128)(2,1)S(1)} %slice.9), channel_id=1, source_target_pairs={{0,96},{16,112},{32,64},{48,80},{64,32},{80,48},{96,0},{112,16},{1... | collective-permute-start | bytes 786440 | tf_op jit(solution)/shard_map/ppermute | solution.py:115
  80.6 1.1 constant_dynamic-update-slice_fusion.5
  81.8 1.6 collective-permute-done.6
  83.4 4.5 %collective-permute-done.7 = bf16[2,64,1024]{2,1,0:T(8,128)(2,1)S(1)} collective-permute-done((bf16[2,64,1024]{2,1,0:T(8,128)(2,1)S(1)}, bf16[2,64,1024]{2,1,0:T(8,128)(2,1)S(1)}, u32[]{:S(2)}, u32[]{:S(2)}) %collective-permute-start.7) | collective-permute-done | bytes 262176 | tf_op jit(solution)/shard_map/ppermute | solution.py:115
  88.0 1.9 %collective-permute-start.8 = (bf16[16,64,1024]{2,1,0:T(8,128)(2,1)S(1)}, bf16[16,64,1024]{2,1,0:T(8,128)(2,1)}, u32[]{:S(2)}, u32[]{:S(2)}) collective-permute-start(bf16[16,64,1024]{2,1,0:T(8,128)(2,1)S(1)} %constant_dynamic-update-slice_fusion.2), channel_id=1, source_target_pairs={{0,16},{16,0},{32,48},{48,32},{64,80},{80,64},{96,112},{112,96},{1... | collective-permute-start | bytes 6291464 | tf_op jit(solution)/shard_map/ppermute | solution.py:119
  89.9 2.5 %broadcast_in_dim.27 = bf16[32,64,1024]{2,1,0:T(8,128)(2,1)} broadcast(bf16[]{:T(256)} %constant.64.clone.1), dimensions={} | broadcast | bytes 4194306 | tf_op jit(solution)/shard_map/broadcast_in_dim | solution.py:120
  92.4 1.6 constant_dynamic-update-slice_fusion.1
  94.0 0.2 collective-permute-done.8
  94.1 3.1 %constant_dynamic-update-slice_fusion = bf16[32,64,1024]{2,1,0:T(8,128)(2,1)} fusion(bf16[32,64,1024]{2,1,0:T(8,128)(2,1)} %constant_dynamic-update-slice_fusion.1, bf16[16,64,1024]{2,1,0:T(8,128)(2,1)} %collective-permute-done.8, s32[]{:T(128)S(6)} %select_n.65), kind=kLoop, calls=%fused_computation.7 | loop fusion | bytes 4194308 | tf_op jit(solution)/shard_map/dynamic_update_slice | solution.py:122
  97.3 6.3 %copy.7 = bf16[4,1024,512]{2,1,0:T(8,128)(2,1)} copy(bf16[4,1024,512]{1,2,0:T(8,128)(2,1)} %bitcast.6) | data formatting | bytes 8388608 | tf_op jit(solution)/shard_map/transpose | solution.py:123
  103.5 16.9 %all-gather.3.cloned.1.call-done = bf16[16384,256]{1,0:T(8,128)(2,1)} async-done(((bf16[1024,256]{1,0:T(8,128)(2,1)}), bf16[16384,256]{1,0:T(8,128)(2,1)}) %all-gather.3.cloned.1.call-update) | async-done | bytes 8388624 | tf_op jit(solution)/shard_map/all_gather | solution.py:105
  120.4 9.6 %shard_map.68 = (f32[1024,512]{1,0:T(8,128)}, f32[16,8,128]{2,1,0:T(8,128)}) custom-call(s32[1]{0:T(128)} %bitcast.z_ref, bf16[1024,512]{1,0:T(8,128)(2,1)} %base_ref.1, bf16[4096,512]{1,0:T(8,128)(2,1)} %bitcast.16, bf16[16,1024,256]{2,1,0:T(8,128)(2,1)} %bitcast.17), custom_call_target="tpu_custom_call" | custom-call | flops 4294967296 | bytes 15728640 | tf_op jit(solution)/shard_map/pallas_call | solution.py:69
  130.0 14.4 %all-to-all-start = ((f32[16,8,128]{2,1,0:T(8,128)}), f32[16,8,128]{2,1,0:T(8,128)S(1)}, u32[]{:S(2)}, u32[]{:S(2)}) async-start(f32[16,8,128]{2,1,0:T(8,128)} %get-tuple-element.5), calls=%async_computation | async-start | bytes 131072 | tf_op jit(solution)/shard_map/all_to_all | solution.py:126
  144.4 13.0 %all-to-all-done = f32[16,8,128]{2,1,0:T(8,128)S(1)} async-done(((f32[16,8,128]{2,1,0:T(8,128)}), f32[16,8,128]{2,1,0:T(8,128)S(1)}, u32[]{:S(2)}, u32[]{:S(2)}) %all-to-all-start) | async-done | bytes 65568 | tf_op jit(solution)/shard_map/all_to_all | solution.py:126
  157.4 2.8 %multiply_convert_fusion = bf16[1024,512]{1,0:T(8,128)(2,1)} fusion(f32[1024,512]{1,0:T(8,128)} %get-tuple-element.4, f32[512]{0:T(512)S(1)} %convert_element_type.14, f32[1024]{0:T(1024)S(1)} %rsqrt_bitcast_fusion), kind=kLoop, calls=%fused_computation | loop fusion | flops 1572864 | bytes 3151872 | tf_op jit(solution)/shard_map/convert_element_type | solution.py:130
  (16 shorter events, 0.2 us)
Async XLA Ops:
  7.2 113.2 %all-gather.3.cloned.1.call-start = ((), (), s32[]{:S(2)}) async-start(), calls=%async_computation.1 | async-start | bytes 8912896 | tf_op jit(solution)/shard_map/all_gather | solution.py:105
  9.6 18.9 %collective-permute-start = (bf16[64,1024]{1,0:T(8,128)(2,1)S(1)}, bf16[64,1024]{1,0:T(8,128)(2,1)S(1)}, u32[]{:S(2)}, u32[]{:S(2)}) collective-permute-start(bf16[64,1024]{1,0:T(8,128)(2,1)S(1)} %get-tuple-element.6), channel_id=1, source_target_pairs={{0,0},{4,80},{8,16},{12,64},{16,128},{20,208},{24,144},{28,192},{3... | collective-permute-start | bytes 393224 | tf_op jit(solution)/shard_map/ppermute | solution.py:106
  28.5 22.8 %collective-permute-start.1 = (bf16[64,1024]{1,0:T(8,128)(2,1)S(1)}, bf16[64,1024]{1,0:T(8,128)(2,1)S(1)}, u32[]{:S(2)}, u32[]{:S(2)}) collective-permute-start(bf16[64,1024]{1,0:T(8,128)(2,1)S(1)} %collective-permute-done), channel_id=1, source_target_pairs={{0,128},{16,144},{32,160},{48,176},{64,192},{80,208},{96,224},{112... | collective-permute-start | bytes 393224 | tf_op jit(solution)/shard_map/ppermute | solution.py:110
  45.9 8.5 %collective-permute-start.2 = (bf16[64,1024]{1,0:T(8,128)(2,1)S(1)}, bf16[64,1024]{1,0:T(8,128)(2,1)S(1)}, u32[]{:S(2)}, u32[]{:S(2)}) collective-permute-start(bf16[64,1024]{1,0:T(8,128)(2,1)S(1)} %collective-permute-done), channel_id=1, source_target_pairs={{0,256},{16,272},{32,288},{48,304},{64,320},{80,336},{96,352},{112... | collective-permute-start | bytes 393224 | tf_op jit(solution)/shard_map/ppermute | solution.py:110
  47.9 9.3 %collective-permute-start.3 = (bf16[64,1024]{1,0:T(8,128)(2,1)S(1)}, bf16[64,1024]{1,0:T(8,128)(2,1)S(1)}, u32[]{:S(2)}, u32[]{:S(2)}) collective-permute-start(bf16[64,1024]{1,0:T(8,128)(2,1)S(1)} %collective-permute-done), channel_id=1, source_target_pairs={{0,384},{16,400},{32,416},{48,432},{64,448},{80,464},{96,480},{112... | collective-permute-start | bytes 393224 | tf_op jit(solution)/shard_map/ppermute | solution.py:110
  57.2 16.3 %collective-permute-start.5 = (bf16[4,64,1024]{2,1,0:T(8,128)(2,1)S(1)}, bf16[4,64,1024]{2,1,0:T(8,128)(2,1)S(1)}, u32[]{:S(2)}, u32[]{:S(2)}) collective-permute-start(bf16[4,64,1024]{2,1,0:T(8,128)(2,1)S(1)} %bitcast_dynamic-update-slice_fusion), channel_id=1, source_target_pairs={{0,96},{16,112},{32,64},{48,80},{64,32},{80,48},{96,0},{112,16},{1... | collective-permute-start | bytes 1572872 | tf_op jit(solution)/shard_map/ppermute | solution.py:113
  61.2 16.5 %collective-permute-start.4 = (bf16[4,64,1024]{2,1,0:T(8,128)(2,1)S(1)}, bf16[4,64,1024]{2,1,0:T(8,128)(2,1)}, u32[]{:S(2)}, u32[]{:S(2)}) collective-permute-start(bf16[4,64,1024]{2,1,0:T(8,128)(2,1)S(1)} %bitcast_dynamic-update-slice_fusion), channel_id=1, source_target_pairs={{0,32},{16,48},{32,0},{48,16},{64,96},{80,112},{96,64},{112,80},{1... | collective-permute-start | bytes 1572872 | tf_op jit(solution)/shard_map/ppermute | solution.py:112
  73.5 9.9 %collective-permute-start.6 = (bf16[2,64,1024]{2,1,0:T(8,128)(2,1)S(1)}, bf16[2,64,1024]{2,1,0:T(8,128)(2,1)S(1)}, u32[]{:S(2)}, u32[]{:S(2)}) collective-permute-start(bf16[2,64,1024]{2,1,0:T(8,128)(2,1)S(1)} %slice.8), channel_id=1, source_target_pairs={{0,32},{16,48},{32,0},{48,16},{64,96},{80,112},{96,64},{112,80},{1... | collective-permute-start | bytes 786440 | tf_op jit(solution)/shard_map/ppermute | solution.py:114
  78.7 9.2 %collective-permute-start.7 = (bf16[2,64,1024]{2,1,0:T(8,128)(2,1)S(1)}, bf16[2,64,1024]{2,1,0:T(8,128)(2,1)S(1)}, u32[]{:S(2)}, u32[]{:S(2)}) collective-permute-start(bf16[2,64,1024]{2,1,0:T(8,128)(2,1)S(1)} %slice.9), channel_id=1, source_target_pairs={{0,96},{16,112},{32,64},{48,80},{64,32},{80,48},{96,0},{112,16},{1... | collective-permute-start | bytes 786440 | tf_op jit(solution)/shard_map/ppermute | solution.py:115
  88.0 6.2 %collective-permute-start.8 = (bf16[16,64,1024]{2,1,0:T(8,128)(2,1)S(1)}, bf16[16,64,1024]{2,1,0:T(8,128)(2,1)}, u32[]{:S(2)}, u32[]{:S(2)}) collective-permute-start(bf16[16,64,1024]{2,1,0:T(8,128)(2,1)S(1)} %constant_dynamic-update-slice_fusion.2), channel_id=1, source_target_pairs={{0,16},{16,0},{32,48},{48,32},{64,80},{80,64},{96,112},{112,96},{1... | collective-permute-start | bytes 6291464 | tf_op jit(solution)/shard_map/ppermute | solution.py:119
  120.4 24.0 %copy-start = (bf16[512]{0:T(512)(128)(2,1)S(1)}, bf16[512]{0:T(512)(128)(2,1)}, u32[]{:S(2)}) copy-start(bf16[512]{0:T(512)(128)(2,1)} %param.9) | copy-start | bytes 3076
  130.0 27.5 %all-to-all-start = ((f32[16,8,128]{2,1,0:T(8,128)}), f32[16,8,128]{2,1,0:T(8,128)S(1)}, u32[]{:S(2)}, u32[]{:S(2)}) async-start(f32[16,8,128]{2,1,0:T(8,128)} %get-tuple-element.5), calls=%async_computation | async-start | bytes 131072 | tf_op jit(solution)/shard_map/all_to_all | solution.py:126
Sparse Core Ops, SparseCore 0:
  10.1 110.2 all-gather.2

commit v3 on v2

--- a/solution.py
+++ b/solution.py
@@ -16,7 +16,6 @@
 TOK = 1024
 FEAT = 256
 COLS = 512
-TILE = 256
 
 
 def place(f, t, y):
@@ -44,51 +43,62 @@
     return pairs
 
 
-def kernel(z_ref, base_ref, weight_ref, context_ref, out_ref, squares_ref):
-    part = pl.program_id(0)
+def kernel(z_ref, base_hbm, weight_hbm, context_hbm, out_ref, squares_ref, base, weight, context, sems):
     first = z_ref[0] // 4 + z_ref[0] % 4
-    block = jnp.concatenate(
-        [context_ref[(first - turn + 4) % 4 * 4 + i] for turn in range(4) for i in range(4)],
-        axis=1,
-    )
-    total = base_ref[...].astype(jnp.float32) + jnp.dot(
-        block, weight_ref[...], preferred_element_type=jnp.float32
-    )
-    out_ref[...] = total
+    copies = []
+    for turn in range(4):
+        plane = pl.ds((first - turn + 4) % 4 * 4, 4)
+        copies.append(
+            (
+                pltpu.make_async_copy(weight_hbm.at[turn], weight.at[turn], sems.at[2 * turn]),
+                pltpu.make_async_copy(
+                    context_hbm.at[plane], context.at[turn], sems.at[2 * turn + 1]
+                ),
+            )
+        )
+    base_copy = pltpu.make_async_copy(base_hbm, base, sems.at[8])
+    for pair in copies:
+        pair[0].start()
+        pair[1].start()
+    base_copy.start()
+    total = 0
+    for turn, pair in enumerate(copies):
+        pair[0].wait()
+        pair[1].wait()
+        block = jnp.concatenate([context[turn, i] for i in range(4)], axis=1)
+        total += jnp.dot(block, weight[turn], preferred_element_type=jnp.float32)
+    base_copy.wait()
+    total += base[...].astype(jnp.float32)
+    out_ref[...] = total.astype(jnp.bfloat16)
     squared = total * total
     lanes = sum(squared[:, i * 128 : (i + 1) * 128] for i in range(COLS // 128))
     sums = jnp.sum(lanes.T, axis=0, keepdims=True)
-    for i in range(TILE // 128):
-        squares_ref[:, pl.ds(part * (TILE // 128) + i, 1), :] = jnp.broadcast_to(
+    for i in range(TOK // 128):
+        squares_ref[:, i : i + 1, :] = jnp.broadcast_to(
             sums[:, i * 128 : (i + 1) * 128][None], (NZ, 1, 128)
         )
 
 
 def product(z, base, weight, context):
-    row = lambda i, z: (i, 0)
     return pl.pallas_call(
         kernel,
         out_shape=[
-            jax.ShapeDtypeStruct((TOK, COLS), jnp.float32),
+            jax.ShapeDtypeStruct((TOK, COLS), jnp.bfloat16),
             jax.ShapeDtypeStruct((NZ, TOK // 128, 128), jnp.float32),
         ],
-        grid_spec=pltpu.PrefetchScalarGridSpec(
-            num_scalar_prefetch=1,
-            grid=(TOK // TILE,),
-            in_specs=[
-                pl.BlockSpec((TILE, COLS), row),
-                pl.BlockSpec((H, COLS), lambda i, z: (0, 0)),
-                pl.BlockSpec((NZ, TILE, FEAT), lambda i, z: (0, i, 0)),
-            ],
-            out_specs=[
-                pl.BlockSpec((TILE, COLS), row),
-                pl.BlockSpec((NZ, TOK // 128, 128), lambda i, z: (0, 0, 0)),
-            ],
-        ),
-        compiler_params=pltpu.CompilerParams(vmem_limit_bytes=58 * 1024 * 1024),
+        in_specs=[pl.BlockSpec(memory_space=pltpu.SMEM)]
+        + [pl.BlockSpec(memory_space=pltpu.HBM)] * 3,
+        out_specs=[pl.BlockSpec(memory_space=pltpu.VMEM)] * 2,
+        scratch_shapes=[
+            pltpu.VMEM((TOK, COLS), jnp.bfloat16),
+            pltpu.VMEM((4, 1024, COLS), jnp.bfloat16),
+            pltpu.VMEM((4, 4, TOK, FEAT), jnp.bfloat16),
+            pltpu.SemaphoreType.DMA((9,)),
+        ],
+        compiler_params=pltpu.CompilerParams(vmem_limit_bytes=60 * 1024 * 1024),
         cost_estimate=pl.CostEstimate(
             flops=2 * TOK * COLS * H,
-            bytes_accessed=(TOK + COLS) * H * 2 + TOK * COLS * 6,
+            bytes_accessed=(TOK + COLS) * H * 2 + TOK * COLS * 4,
             transcendentals=0,
         ),
     )(z, base, weight, context)
@@ -120,7 +130,7 @@
     pieces = jnp.zeros((32, 64, 1024), jnp.bfloat16)
     pieces = lax.dynamic_update_slice(pieces, plane, (c * 16, 0, 0))
     pieces = lax.dynamic_update_slice(pieces, other, ((1 - c) * 16, 0, 0))
-    weight = pieces.reshape(4, COLS, 1024).transpose(0, 2, 1).reshape(H, COLS)
+    weight = pieces.reshape(4, COLS, 1024).transpose(0, 2, 1)
     hidden, squares = product(z[None], residual, weight, gathered)
 
     totals = jnp.sum(lax.all_to_all(squares, Z, 0, 0, tiled=True), axis=0)

time: 168 us -> 167 us (level)
    reshape x0 -> x1, local copies, waits for them, and re-layouts: none -> 6.25 us  [shards(): weight = pieces.reshape(4, COLS, 1024).transpose(0, 2, 1)]
    transpose x1 -> x0, local copies, waits for them, and re-layouts: 6.25 us -> none  [shards(): weight = pieces.reshape(4, COLS, 1024).transpose(0, 2, 1).reshape(H, COLS)]
where the time goes in v3:
time: 167 us; the launch traced here: 166 us
  starting transfers between devices  66 us (40%)
  waiting for transfers between devices  56.7 us (34%)
  local copies, waits for them, and re-layouts  16 us (10%)
  between operations  14.4 us (9%)
  Pallas kernels  8.82 us (5%)
  other arithmetic  4.27 us (3%)
    ppermute x3, starting transfers between devices, shards(): got = piece if dx == 0 else lax.ppermute(piece, 'fsdp', partner(dx, 0, 0))  22.7 us
    all_gather x1, waiting for transfers between devices, shards(): gathered = lax.all_gather(context, Z, axis=0)  16.9 us
    ppermute x1, starting transfers between devices, shards(): piece = lax.ppermute(recast, ALL, SPREAD)  15 us
    all_to_all x1, starting transfers between devices, shards(): totals = jnp.sum(lax.all_to_all(squares, Z, 0, 0, tiled=True), axis=0)  14.4 us
    all_to_all x1, waiting for transfers between devices, shards(): totals = jnp.sum(lax.all_to_all(squares, Z, 0, 0, tiled=True), axis=0)  13 us
    ppermute x1, waiting for transfers between devices, shards(): back = lax.ppermute(row, 'fsdp', partner(0, 3, 0))  10.3 us
    pallas_call x1, Pallas kernels, product(): pl.pallas_call(kernel, out_shape=[jax.ShapeDtypeStruct((TOK, COLS), jnp.b...  8.82 us
    reshape x1, local copies, waits for them, and re-layouts, shards(): weight = pieces.reshape(4, COLS, 1024).transpose(0, 2, 1)  6.25 us
  transfers between devices with their start and end apart: 11, of which 9 were waited for; matrix products, arithmetic and copies ran while one was open for 11% of the time, Pallas kernels for 0%

profile of v3, /device:TPU:12, one launch (start us, length us, event | category | flops | bytes accessed | tf_op | source)
XLA Modules:
  0.0 166.1 jit_solution(2193058302099449272)
XLA Ops:
  7.2 0.0 all-gather.3.cloned.1.call-start
  7.2 0.7 all-gather.3.cloned.1.call-update
  7.9 1.7 %fusion = (bf16[64,1024]{1,0:T(8,128)(2,1)S(1)}, f32[64,1024]{1,0:T(8,128)}) fusion(f32[64,1024]{1,0:T(8,128)} %param.8, bf16[64,1024]{1,0:T(8,128)(2,1)} %param.7), kind=kLoop, calls=%fused_computation.14 | loop fusion | flops 327680 | bytes 786432 | tf_op jit(solution)/shard_map/convert_element_type | solution.py:109
  9.6 15.0 %collective-permute-start = (bf16[64,1024]{1,0:T(8,128)(2,1)S(1)}, bf16[64,1024]{1,0:T(8,128)(2,1)S(1)}, u32[]{:S(2)}, u32[]{:S(2)}) collective-permute-start(bf16[64,1024]{1,0:T(8,128)(2,1)S(1)} %get-tuple-element.6), channel_id=1, source_target_pairs={{0,0},{4,80},{8,16},{12,64},{16,128},{20,208},{24,144},{28,192},{3... | collective-permute-start | bytes 393224 | tf_op jit(solution)/shard_map/ppermute | solution.py:116
  24.7 3.8 %collective-permute-done = bf16[64,1024]{1,0:T(8,128)(2,1)S(1)} collective-permute-done((bf16[64,1024]{1,0:T(8,128)(2,1)S(1)}, bf16[64,1024]{1,0:T(8,128)(2,1)S(1)}, u32[]{:S(2)}, u32[]{:S(2)}) %collective-permute-start) | collective-permute-done | bytes 131104 | tf_op jit(solution)/shard_map/ppermute | solution.py:116
  28.5 17.4 %collective-permute-start.1 = (bf16[64,1024]{1,0:T(8,128)(2,1)S(1)}, bf16[64,1024]{1,0:T(8,128)(2,1)S(1)}, u32[]{:S(2)}, u32[]{:S(2)}) collective-permute-start(bf16[64,1024]{1,0:T(8,128)(2,1)S(1)} %collective-permute-done), channel_id=1, source_target_pairs={{0,128},{16,144},{32,160},{48,176},{64,192},{80,208},{96,224},{112... | collective-permute-start | bytes 393224 | tf_op jit(solution)/shard_map/ppermute | solution.py:120
  45.9 1.9 %collective-permute-start.2 = (bf16[64,1024]{1,0:T(8,128)(2,1)S(1)}, bf16[64,1024]{1,0:T(8,128)(2,1)S(1)}, u32[]{:S(2)}, u32[]{:S(2)}) collective-permute-start(bf16[64,1024]{1,0:T(8,128)(2,1)S(1)} %collective-permute-done), channel_id=1, source_target_pairs={{0,256},{16,272},{32,288},{48,304},{64,320},{80,336},{96,352},{112... | collective-permute-start | bytes 393224 | tf_op jit(solution)/shard_map/ppermute | solution.py:120
  47.9 3.4 %collective-permute-start.3 = (bf16[64,1024]{1,0:T(8,128)(2,1)S(1)}, bf16[64,1024]{1,0:T(8,128)(2,1)S(1)}, u32[]{:S(2)}, u32[]{:S(2)}) collective-permute-start(bf16[64,1024]{1,0:T(8,128)(2,1)S(1)} %collective-permute-done), channel_id=1, source_target_pairs={{0,384},{16,400},{32,416},{48,432},{64,448},{80,464},{96,480},{112... | collective-permute-start | bytes 393224 | tf_op jit(solution)/shard_map/ppermute | solution.py:120
  51.2 0.1 broadcast_in_dim.29
  51.4 3.1 %collective-permute-done.2 = bf16[64,1024]{1,0:T(8,128)(2,1)S(1)} collective-permute-done((bf16[64,1024]{1,0:T(8,128)(2,1)S(1)}, bf16[64,1024]{1,0:T(8,128)(2,1)S(1)}, u32[]{:S(2)}, u32[]{:S(2)}) %collective-permute-start.2) | collective-permute-done | bytes 131104 | tf_op jit(solution)/shard_map/ppermute | solution.py:120
  54.4 2.7 %collective-permute-done.3 = bf16[64,1024]{1,0:T(8,128)(2,1)S(1)} collective-permute-done((bf16[64,1024]{1,0:T(8,128)(2,1)S(1)}, bf16[64,1024]{1,0:T(8,128)(2,1)S(1)}, u32[]{:S(2)}, u32[]{:S(2)}) %collective-permute-start.3) | collective-permute-done | bytes 131104 | tf_op jit(solution)/shard_map/ppermute | solution.py:120
  57.2 4.0 %collective-permute-start.5 = (bf16[4,64,1024]{2,1,0:T(8,128)(2,1)S(1)}, bf16[4,64,1024]{2,1,0:T(8,128)(2,1)S(1)}, u32[]{:S(2)}, u32[]{:S(2)}) collective-permute-start(bf16[4,64,1024]{2,1,0:T(8,128)(2,1)S(1)} %bitcast_dynamic-update-slice_fusion), channel_id=1, source_target_pairs={{0,96},{16,112},{32,64},{48,80},{64,32},{80,48},{96,0},{112,16},{1... | collective-permute-start | bytes 1572872 | tf_op jit(solution)/shard_map/ppermute | solution.py:123
  61.2 1.9 %collective-permute-start.4 = (bf16[4,64,1024]{2,1,0:T(8,128)(2,1)S(1)}, bf16[4,64,1024]{2,1,0:T(8,128)(2,1)}, u32[]{:S(2)}, u32[]{:S(2)}) collective-permute-start(bf16[4,64,1024]{2,1,0:T(8,128)(2,1)S(1)} %bitcast_dynamic-update-slice_fusion), channel_id=1, source_target_pairs={{0,32},{16,48},{32,0},{48,16},{64,96},{80,112},{96,64},{112,80},{1... | collective-permute-start | bytes 1572872 | tf_op jit(solution)/shard_map/ppermute | solution.py:122
  63.2 10.3 %collective-permute-done.5 = bf16[4,64,1024]{2,1,0:T(8,128)(2,1)S(1)} collective-permute-done((bf16[4,64,1024]{2,1,0:T(8,128)(2,1)S(1)}, bf16[4,64,1024]{2,1,0:T(8,128)(2,1)S(1)}, u32[]{:S(2)}, u32[]{:S(2)}) %collective-permute-start.5) | collective-permute-done | bytes 524320 | tf_op jit(solution)/shard_map/ppermute | solution.py:123
  73.5 3.9 %collective-permute-start.6 = (bf16[2,64,1024]{2,1,0:T(8,128)(2,1)S(1)}, bf16[2,64,1024]{2,1,0:T(8,128)(2,1)S(1)}, u32[]{:S(2)}, u32[]{:S(2)}) collective-permute-start(bf16[2,64,1024]{2,1,0:T(8,128)(2,1)S(1)} %slice.8), channel_id=1, source_target_pairs={{0,32},{16,48},{32,0},{48,16},{64,96},{80,112},{96,64},{112,80},{1... | collective-permute-start | bytes 786440 | tf_op jit(solution)/shard_map/ppermute | solution.py:124
  77.4 0.3 broadcast_in_dim.28
  77.7 1.0 slice.9
  78.7 1.9 %collective-permute-start.7 = (bf16[2,64,1024]{2,1,0:T(8,128)(2,1)S(1)}, bf16[2,64,1024]{2,1,0:T(8,128)(2,1)S(1)}, u32[]{:S(2)}, u32[]{:S(2)}) collective-permute-start(bf16[2,64,1024]{2,1,0:T(8,128)(2,1)S(1)} %slice.9), channel_id=1, source_target_pairs={{0,96},{16,112},{32,64},{48,80},{64,32},{80,48},{96,0},{112,16},{1... | collective-permute-start | bytes 786440 | tf_op jit(solution)/shard_map/ppermute | solution.py:125
  80.6 1.1 constant_dynamic-update-slice_fusion.5
  81.8 1.6 collective-permute-done.6
  83.4 4.5 %collective-permute-done.7 = bf16[2,64,1024]{2,1,0:T(8,128)(2,1)S(1)} collective-permute-done((bf16[2,64,1024]{2,1,0:T(8,128)(2,1)S(1)}, bf16[2,64,1024]{2,1,0:T(8,128)(2,1)S(1)}, u32[]{:S(2)}, u32[]{:S(2)}) %collective-permute-start.7) | collective-permute-done | bytes 262176 | tf_op jit(solution)/shard_map/ppermute | solution.py:125
  88.0 1.9 %collective-permute-start.8 = (bf16[16,64,1024]{2,1,0:T(8,128)(2,1)S(1)}, bf16[16,64,1024]{2,1,0:T(8,128)(2,1)}, u32[]{:S(2)}, u32[]{:S(2)}) collective-permute-start(bf16[16,64,1024]{2,1,0:T(8,128)(2,1)S(1)} %constant_dynamic-update-slice_fusion.2), channel_id=1, source_target_pairs={{0,16},{16,0},{32,48},{48,32},{64,80},{80,64},{96,112},{112,96},{1... | collective-permute-start | bytes 6291464 | tf_op jit(solution)/shard_map/ppermute | solution.py:129
  89.9 2.5 %broadcast_in_dim.27 = bf16[32,64,1024]{2,1,0:T(8,128)(2,1)} broadcast(bf16[]{:T(256)} %constant.64.clone.1), dimensions={} | broadcast | bytes 4194306 | tf_op jit(solution)/shard_map/broadcast_in_dim | solution.py:130
  92.4 1.6 constant_dynamic-update-slice_fusion.1
  94.0 0.2 collective-permute-done.8
  94.1 3.1 %constant_dynamic-update-slice_fusion = bf16[32,64,1024]{2,1,0:T(8,128)(2,1)} fusion(bf16[32,64,1024]{2,1,0:T(8,128)(2,1)} %constant_dynamic-update-slice_fusion.1, bf16[16,64,1024]{2,1,0:T(8,128)(2,1)} %collective-permute-done.8, s32[]{:T(128)S(6)} %select_n.65), kind=kLoop, calls=%fused_computation.7 | loop fusion | bytes 4194308 | tf_op jit(solution)/shard_map/dynamic_update_slice | solution.py:132
  97.3 6.3 %copy.7 = bf16[4,512,1024]{1,2,0:T(8,128)(2,1)} copy(bf16[4,512,1024]{2,1,0:T(8,128)(2,1)} %bitcast.5) | data formatting | bytes 8388608 | tf_op jit(solution)/shard_map/reshape | solution.py:133
  103.5 16.9 %all-gather.3.cloned.1.call-done = bf16[16384,256]{1,0:T(8,128)(2,1)} async-done(((bf16[1024,256]{1,0:T(8,128)(2,1)}), bf16[16384,256]{1,0:T(8,128)(2,1)}) %all-gather.3.cloned.1.call-update) | async-done | bytes 8388624 | tf_op jit(solution)/shard_map/all_gather | solution.py:115
  120.4 8.8 %shard_map.68 = (bf16[1024,512]{1,0:T(8,128)(2,1)}, f32[16,8,128]{2,1,0:T(8,128)}) custom-call(s32[1]{0:T(128)} %bitcast.z_ref, bf16[1024,512]{1,0:T(8,128)(2,1)} %base_hbm.1, bf16[4,1024,512]{2,1,0:T(8,128)(2,1)} %bitcast.14, bf16[16,1024,256]{2,1,0:T(8,128)(2,1)} %bitcast.15), custom_call_target="tpu_custom_call" | custom-call | flops 4294967296 | bytes 14680064 | tf_op jit(solution)/shard_map/pallas_call | solution.py:83
  129.2 14.4 %all-to-all-start = ((f32[16,8,128]{2,1,0:T(8,128)}), f32[16,8,128]{2,1,0:T(8,128)S(1)}, u32[]{:S(2)}, u32[]{:S(2)}) async-start(f32[16,8,128]{2,1,0:T(8,128)} %get-tuple-element.5), calls=%async_computation | async-start | bytes 131072 | tf_op jit(solution)/shard_map/all_to_all | solution.py:136
  143.7 13.0 %all-to-all-done = f32[16,8,128]{2,1,0:T(8,128)S(1)} async-done(((f32[16,8,128]{2,1,0:T(8,128)}), f32[16,8,128]{2,1,0:T(8,128)S(1)}, u32[]{:S(2)}, u32[]{:S(2)}) %all-to-all-start) | async-done | bytes 65568 | tf_op jit(solution)/shard_map/all_to_all | solution.py:136
  156.7 2.5 %multiply_convert_fusion = bf16[1024,512]{1,0:T(8,128)(2,1)} fusion(bf16[1024,512]{1,0:T(8,128)(2,1)} %get-tuple-element.4, f32[512]{0:T(512)S(1)} %convert_element_type.18, f32[1024]{0:T(1024)S(1)} %rsqrt_bitcast_fusion), kind=kLoop, calls=%fused_computation | loop fusion | flops 2097152 | bytes 2103296 | tf_op jit(solution)/shard_map/convert_element_type | solution.py:140
  (16 shorter events, 0.2 us)
Async XLA Ops:
  7.2 113.2 %all-gather.3.cloned.1.call-start = ((), (), s32[]{:S(2)}) async-start(), calls=%async_computation.1 | async-start | bytes 8912896 | tf_op jit(solution)/shard_map/all_gather | solution.py:115
  9.6 18.9 %collective-permute-start = (bf16[64,1024]{1,0:T(8,128)(2,1)S(1)}, bf16[64,1024]{1,0:T(8,128)(2,1)S(1)}, u32[]{:S(2)}, u32[]{:S(2)}) collective-permute-start(bf16[64,1024]{1,0:T(8,128)(2,1)S(1)} %get-tuple-element.6), channel_id=1, source_target_pairs={{0,0},{4,80},{8,16},{12,64},{16,128},{20,208},{24,144},{28,192},{3... | collective-permute-start | bytes 393224 | tf_op jit(solution)/shard_map/ppermute | solution.py:116
  28.5 22.8 %collective-permute-start.1 = (bf16[64,1024]{1,0:T(8,128)(2,1)S(1)}, bf16[64,1024]{1,0:T(8,128)(2,1)S(1)}, u32[]{:S(2)}, u32[]{:S(2)}) collective-permute-start(bf16[64,1024]{1,0:T(8,128)(2,1)S(1)} %collective-permute-done), channel_id=1, source_target_pairs={{0,128},{16,144},{32,160},{48,176},{64,192},{80,208},{96,224},{112... | collective-permute-start | bytes 393224 | tf_op jit(solution)/shard_map/ppermute | solution.py:120
  45.9 8.5 %collective-permute-start.2 = (bf16[64,1024]{1,0:T(8,128)(2,1)S(1)}, bf16[64,1024]{1,0:T(8,128)(2,1)S(1)}, u32[]{:S(2)}, u32[]{:S(2)}) collective-permute-start(bf16[64,1024]{1,0:T(8,128)(2,1)S(1)} %collective-permute-done), channel_id=1, source_target_pairs={{0,256},{16,272},{32,288},{48,304},{64,320},{80,336},{96,352},{112... | collective-permute-start | bytes 393224 | tf_op jit(solution)/shard_map/ppermute | solution.py:120
  47.9 9.3 %collective-permute-start.3 = (bf16[64,1024]{1,0:T(8,128)(2,1)S(1)}, bf16[64,1024]{1,0:T(8,128)(2,1)S(1)}, u32[]{:S(2)}, u32[]{:S(2)}) collective-permute-start(bf16[64,1024]{1,0:T(8,128)(2,1)S(1)} %collective-permute-done), channel_id=1, source_target_pairs={{0,384},{16,400},{32,416},{48,432},{64,448},{80,464},{96,480},{112... | collective-permute-start | bytes 393224 | tf_op jit(solution)/shard_map/ppermute | solution.py:120
  57.2 16.3 %collective-permute-start.5 = (bf16[4,64,1024]{2,1,0:T(8,128)(2,1)S(1)}, bf16[4,64,1024]{2,1,0:T(8,128)(2,1)S(1)}, u32[]{:S(2)}, u32[]{:S(2)}) collective-permute-start(bf16[4,64,1024]{2,1,0:T(8,128)(2,1)S(1)} %bitcast_dynamic-update-slice_fusion), channel_id=1, source_target_pairs={{0,96},{16,112},{32,64},{48,80},{64,32},{80,48},{96,0},{112,16},{1... | collective-permute-start | bytes 1572872 | tf_op jit(solution)/shard_map/ppermute | solution.py:123
  61.2 16.5 %collective-permute-start.4 = (bf16[4,64,1024]{2,1,0:T(8,128)(2,1)S(1)}, bf16[4,64,1024]{2,1,0:T(8,128)(2,1)}, u32[]{:S(2)}, u32[]{:S(2)}) collective-permute-start(bf16[4,64,1024]{2,1,0:T(8,128)(2,1)S(1)} %bitcast_dynamic-update-slice_fusion), channel_id=1, source_target_pairs={{0,32},{16,48},{32,0},{48,16},{64,96},{80,112},{96,64},{112,80},{1... | collective-permute-start | bytes 1572872 | tf_op jit(solution)/shard_map/ppermute | solution.py:122
  73.5 9.9 %collective-permute-start.6 = (bf16[2,64,1024]{2,1,0:T(8,128)(2,1)S(1)}, bf16[2,64,1024]{2,1,0:T(8,128)(2,1)S(1)}, u32[]{:S(2)}, u32[]{:S(2)}) collective-permute-start(bf16[2,64,1024]{2,1,0:T(8,128)(2,1)S(1)} %slice.8), channel_id=1, source_target_pairs={{0,32},{16,48},{32,0},{48,16},{64,96},{80,112},{96,64},{112,80},{1... | collective-permute-start | bytes 786440 | tf_op jit(solution)/shard_map/ppermute | solution.py:124
  78.7 9.2 %collective-permute-start.7 = (bf16[2,64,1024]{2,1,0:T(8,128)(2,1)S(1)}, bf16[2,64,1024]{2,1,0:T(8,128)(2,1)S(1)}, u32[]{:S(2)}, u32[]{:S(2)}) collective-permute-start(bf16[2,64,1024]{2,1,0:T(8,128)(2,1)S(1)} %slice.9), channel_id=1, source_target_pairs={{0,96},{16,112},{32,64},{48,80},{64,32},{80,48},{96,0},{112,16},{1... | collective-permute-start | bytes 786440 | tf_op jit(solution)/shard_map/ppermute | solution.py:125
  88.0 6.2 %collective-permute-start.8 = (bf16[16,64,1024]{2,1,0:T(8,128)(2,1)S(1)}, bf16[16,64,1024]{2,1,0:T(8,128)(2,1)}, u32[]{:S(2)}, u32[]{:S(2)}) collective-permute-start(bf16[16,64,1024]{2,1,0:T(8,128)(2,1)S(1)} %constant_dynamic-update-slice_fusion.2), channel_id=1, source_target_pairs={{0,16},{16,0},{32,48},{48,32},{64,80},{80,64},{96,112},{112,96},{1... | collective-permute-start | bytes 6291464 | tf_op jit(solution)/shard_map/ppermute | solution.py:129
  120.4 23.3 %copy-start = (bf16[512]{0:T(512)(128)(2,1)S(1)}, bf16[512]{0:T(512)(128)(2,1)}, u32[]{:S(2)}) copy-start(bf16[512]{0:T(512)(128)(2,1)} %param.9) | copy-start | bytes 3076
  129.2 27.5 %all-to-all-start = ((f32[16,8,128]{2,1,0:T(8,128)}), f32[16,8,128]{2,1,0:T(8,128)S(1)}, u32[]{:S(2)}, u32[]{:S(2)}) async-start(f32[16,8,128]{2,1,0:T(8,128)} %get-tuple-element.5), calls=%async_computation | async-start | bytes 131072 | tf_op jit(solution)/shard_map/all_to_all | solution.py:136
Sparse Core Ops, SparseCore 0:
  10.1 110.2 all-gather.2

commit v4 on v3

--- a/solution.py
+++ b/solution.py
@@ -27,11 +27,18 @@
 
 
 SPREAD = []
+LIFT = []
+LIFT_ON = []
 for y in range(4):
     for u in range(4):
         for r in range(8):
             for t in range(4):
-                SPREAD.append((place(8 * u + r, t, y), place(column(r, (u - t + y) % 4), u, y)))
+                there = column(r, (u - t + y) % 4)
+                SPREAD.append((place(8 * u + r, t, y), place(there, t, y)))
+                step = (0, 1, 1 - 2 * (there % 2), -1)[(u - t) % 4]
+                middle = (t + step) % 4
+                LIFT.append((place(there, t, y), place(there, middle, y)))
+                LIFT_ON.append((place(there, middle, y), place(there, u, y)))
 
 
 def partner(dx, dy, dc):
@@ -113,7 +120,9 @@
     x, y, c = f // 8, (f // 2) % 4, f % 2
 
     gathered = lax.all_gather(context, Z, axis=0)
-    piece = lax.ppermute(recast, ALL, SPREAD)
+    piece = recast
+    for pairs in (SPREAD, LIFT, LIFT_ON):
+        piece = lax.ppermute(piece, ALL, pairs)
 
     row = jnp.zeros((4, 64, 1024), jnp.bfloat16)
     for dx in range(4):

time: 167 us -> 165 us (0.988)
  starting transfers between devices: 66 us -> 61.2 us
  waiting for transfers between devices: 56.7 us -> 59.8 us
    ppermute x1, starting transfers between devices: 4.04 us -> 19.3 us  [shards(): back = lax.ppermute(row, 'fsdp', partner(0, 3, 0))]
    ppermute x3, starting transfers between devices: 22.7 us -> 9.21 us  [shards(): got = piece if dx == 0 else lax.ppermute(piece, 'fsdp', partner(dx, 0, 0))]
    ppermute x1 -> x3, starting transfers between devices: 15 us -> 3.23 us  [shards(): piece = lax.ppermute(piece, ALL, pairs)]
    ppermute x1, starting transfers between devices: 1.92 us -> 11.5 us  [shards(): other = lax.ppermute(plane, 'fsdp', partner(0, 0, 1))]
    all_gather x1, waiting for transfers between devices: 16.9 us -> 22.6 us  [shards(): gathered = lax.all_gather(context, Z, axis=0)]
    ppermute x1, waiting for transfers between devices: 10.3 us -> 4.61 us  [shards(): back = lax.ppermute(row, 'fsdp', partner(0, 3, 0))]
    ppermute x1 -> x3, waiting for transfers between devices: 3.77 us -> 8.85 us  [shards(): piece = lax.ppermute(piece, ALL, pairs)]
    all_to_all x1, starting transfers between devices: 14.4 us -> 9.66 us  [shards(): totals = jnp.sum(lax.all_to_all(squares, Z, 0, 0, tiled=True), axis=0)]
  transfers between devices with their start and end apart: 11 -> 13, of which waited for: 9 -> 8; matrix products, arithmetic and copies ran while one was open for 11% -> 11% of each run, Pallas kernels for 0% -> 0%
where the time goes in v4:
time: 165 us
  starting transfers between devices  61.2 us (37%)
  waiting for transfers between devices  59.8 us (36%)
  local copies, waits for them, and re-layouts  16.1 us (10%)
  between operations  14.4 us (9%)
  Pallas kernels  8.81 us (5%)
  other arithmetic  4.26 us (3%)
    all_gather x1, waiting for transfers between devices, shards(): gathered = lax.all_gather(context, Z, axis=0)  22.6 us
    ppermute x1, starting transfers between devices, shards(): back = lax.ppermute(row, 'fsdp', partner(0, 3, 0))  19.3 us
    all_to_all x1, waiting for transfers between devices, shards(): totals = jnp.sum(lax.all_to_all(squares, Z, 0, 0, tiled=True), axis=0)  13 us
    ppermute x1, starting transfers between devices, shards(): other = lax.ppermute(plane, 'fsdp', partner(0, 0, 1))  11.5 us
    all_to_all x1, starting transfers between devices, shards(): totals = jnp.sum(lax.all_to_all(squares, Z, 0, 0, tiled=True), axis=0)  9.66 us
    ppermute x3, starting transfers between devices, shards(): got = piece if dx == 0 else lax.ppermute(piece, 'fsdp', partner(dx, 0, 0))  9.21 us
    ppermute x3, waiting for transfers between devices, shards(): piece = lax.ppermute(piece, ALL, pairs)  8.85 us
    pallas_call x1, Pallas kernels, product(): pl.pallas_call(kernel, out_shape=[jax.ShapeDtypeStruct((TOK, COLS), jnp.b...  8.81 us
  transfers between devices with their start and end apart: 13, of which 8 were waited for; matrix products, arithmetic and copies ran while one was open for 11% of the time, Pallas kernels for 0%

profile of v4, /device:TPU:12, one launch (start us, length us, event | category | flops | bytes accessed | tf_op | source)
XLA Modules:
  0.0 164.5 jit_solution(216469491687484152)
XLA Ops:
  7.2 0.7 all-gather.3.cloned.1.call-update
  7.9 1.7 %fusion = (bf16[64,1024]{1,0:T(8,128)(2,1)S(1)}, f32[64,1024]{1,0:T(8,128)}) fusion(f32[64,1024]{1,0:T(8,128)} %param.8, bf16[64,1024]{1,0:T(8,128)(2,1)} %param.7), kind=kLoop, calls=%fused_computation.14 | loop fusion | flops 327680 | bytes 786432 | tf_op jit(solution)/shard_map/convert_element_type | solution.py:116
  9.6 1.9 %collective-permute-start = (bf16[64,1024]{1,0:T(8,128)(2,1)S(1)}, bf16[64,1024]{1,0:T(8,128)(2,1)S(1)}, u32[]{:S(2)}, u32[]{:S(2)}) collective-permute-start(bf16[64,1024]{1,0:T(8,128)(2,1)S(1)} %get-tuple-element.6), channel_id=1, source_target_pairs={{0,0},{4,84},{8,24},{12,76},{16,128},{20,212},{24,152},{28,204},{3... | collective-permute-start | bytes 393224 | tf_op jit(solution)/shard_map/ppermute | solution.py:125
  11.5 8.8 %collective-permute-done = bf16[64,1024]{1,0:T(8,128)(2,1)S(1)} collective-permute-done((bf16[64,1024]{1,0:T(8,128)(2,1)S(1)}, bf16[64,1024]{1,0:T(8,128)(2,1)S(1)}, u32[]{:S(2)}, u32[]{:S(2)}) %collective-permute-start) | collective-permute-done | bytes 131104 | tf_op jit(solution)/shard_map/ppermute | solution.py:125
  20.4 0.7 collective-permute-start.1
  21.1 0.7 collective-permute-start.2
  21.8 3.3 %collective-permute-start.3 = (bf16[64,1024]{1,0:T(8,128)(2,1)S(1)}, bf16[64,1024]{1,0:T(8,128)(2,1)S(1)}, u32[]{:S(2)}, u32[]{:S(2)}) collective-permute-start(bf16[64,1024]{1,0:T(8,128)(2,1)S(1)} %collective-permute-done.2), channel_id=1, source_target_pairs={{0,128},{16,144},{32,160},{48,176},{64,192},{80,208},{96,224},{112... | collective-permute-start | bytes 393224 | tf_op jit(solution)/shard_map/ppermute | solution.py:129
  25.1 1.9 %collective-permute-start.4 = (bf16[64,1024]{1,0:T(8,128)(2,1)S(1)}, bf16[64,1024]{1,0:T(8,128)(2,1)S(1)}, u32[]{:S(2)}, u32[]{:S(2)}) collective-permute-start(bf16[64,1024]{1,0:T(8,128)(2,1)S(1)} %collective-permute-done.2), channel_id=1, source_target_pairs={{0,256},{16,272},{32,288},{48,304},{64,320},{80,336},{96,352},{112... | collective-permute-start | bytes 393224 | tf_op jit(solution)/shard_map/ppermute | solution.py:129
  27.0 4.0 %collective-permute-start.5 = (bf16[64,1024]{1,0:T(8,128)(2,1)S(1)}, bf16[64,1024]{1,0:T(8,128)(2,1)S(1)}, u32[]{:S(2)}, u32[]{:S(2)}) collective-permute-start(bf16[64,1024]{1,0:T(8,128)(2,1)S(1)} %collective-permute-done.2), channel_id=1, source_target_pairs={{0,384},{16,400},{32,416},{48,432},{64,448},{80,464},{96,480},{112... | collective-permute-start | bytes 393224 | tf_op jit(solution)/shard_map/ppermute | solution.py:129
  31.0 0.1 broadcast_in_dim.29
  31.1 2.4 %collective-permute-done.4 = bf16[64,1024]{1,0:T(8,128)(2,1)S(1)} collective-permute-done((bf16[64,1024]{1,0:T(8,128)(2,1)S(1)}, bf16[64,1024]{1,0:T(8,128)(2,1)S(1)}, u32[]{:S(2)}, u32[]{:S(2)}) %collective-permute-start.4) | collective-permute-done | bytes 131104 | tf_op jit(solution)/shard_map/ppermute | solution.py:129
  33.5 1.3 collective-permute-done.5
  34.8 19.3 %collective-permute-start.7 = (bf16[4,64,1024]{2,1,0:T(8,128)(2,1)S(1)}, bf16[4,64,1024]{2,1,0:T(8,128)(2,1)S(1)}, u32[]{:S(2)}, u32[]{:S(2)}) collective-permute-start(bf16[4,64,1024]{2,1,0:T(8,128)(2,1)S(1)} %bitcast_dynamic-update-slice_fusion), channel_id=1, source_target_pairs={{0,96},{16,112},{32,64},{48,80},{64,32},{80,48},{96,0},{112,16},{1... | collective-permute-start | bytes 1572872 | tf_op jit(solution)/shard_map/ppermute | solution.py:132
  54.2 2.5 %collective-permute-start.6 = (bf16[4,64,1024]{2,1,0:T(8,128)(2,1)S(1)}, bf16[4,64,1024]{2,1,0:T(8,128)(2,1)}, u32[]{:S(2)}, u32[]{:S(2)}) collective-permute-start(bf16[4,64,1024]{2,1,0:T(8,128)(2,1)S(1)} %bitcast_dynamic-update-slice_fusion), channel_id=1, source_target_pairs={{0,32},{16,48},{32,0},{48,16},{64,96},{80,112},{96,64},{112,80},{1... | collective-permute-start | bytes 1572872 | tf_op jit(solution)/shard_map/ppermute | solution.py:131
  56.7 4.6 %collective-permute-done.7 = bf16[4,64,1024]{2,1,0:T(8,128)(2,1)S(1)} collective-permute-done((bf16[4,64,1024]{2,1,0:T(8,128)(2,1)S(1)}, bf16[4,64,1024]{2,1,0:T(8,128)(2,1)S(1)}, u32[]{:S(2)}, u32[]{:S(2)}) %collective-permute-start.7) | collective-permute-done | bytes 524320 | tf_op jit(solution)/shard_map/ppermute | solution.py:132
  61.3 2.5 %collective-permute-start.8 = (bf16[2,64,1024]{2,1,0:T(8,128)(2,1)S(1)}, bf16[2,64,1024]{2,1,0:T(8,128)(2,1)S(1)}, u32[]{:S(2)}, u32[]{:S(2)}) collective-permute-start(bf16[2,64,1024]{2,1,0:T(8,128)(2,1)S(1)} %slice.8), channel_id=1, source_target_pairs={{0,32},{16,48},{32,0},{48,16},{64,96},{80,112},{96,64},{112,80},{1... | collective-permute-start | bytes 786440 | tf_op jit(solution)/shard_map/ppermute | solution.py:133
  63.8 0.3 broadcast_in_dim.28
  64.1 1.2 collective-permute-done.6
  65.4 1.0 slice.9
  66.3 3.3 %collective-permute-start.9 = (bf16[2,64,1024]{2,1,0:T(8,128)(2,1)S(1)}, bf16[2,64,1024]{2,1,0:T(8,128)(2,1)S(1)}, u32[]{:S(2)}, u32[]{:S(2)}) collective-permute-start(bf16[2,64,1024]{2,1,0:T(8,128)(2,1)S(1)} %slice.9), channel_id=1, source_target_pairs={{0,96},{16,112},{32,64},{48,80},{64,32},{80,48},{96,0},{112,16},{1... | collective-permute-start | bytes 786440 | tf_op jit(solution)/shard_map/ppermute | solution.py:134
  69.6 1.1 constant_dynamic-update-slice_fusion.5
  70.8 5.2 %collective-permute-done.9 = bf16[2,64,1024]{2,1,0:T(8,128)(2,1)S(1)} collective-permute-done((bf16[2,64,1024]{2,1,0:T(8,128)(2,1)S(1)}, bf16[2,64,1024]{2,1,0:T(8,128)(2,1)S(1)}, u32[]{:S(2)}, u32[]{:S(2)}) %collective-permute-start.9) | collective-permute-done | bytes 262176 | tf_op jit(solution)/shard_map/ppermute | solution.py:134
  76.1 11.5 %collective-permute-start.10 = (bf16[16,64,1024]{2,1,0:T(8,128)(2,1)S(1)}, bf16[16,64,1024]{2,1,0:T(8,128)(2,1)}, u32[]{:S(2)}, u32[]{:S(2)}) collective-permute-start(bf16[16,64,1024]{2,1,0:T(8,128)(2,1)S(1)} %constant_dynamic-update-slice_fusion.2), channel_id=1, source_target_pairs={{0,16},{16,0},{32,48},{48,32},{64,80},{80,64},{96,112},{112,96},{1... | collective-permute-start | bytes 6291464 | tf_op jit(solution)/shard_map/ppermute | solution.py:138
  87.6 2.5 %broadcast_in_dim.27 = bf16[32,64,1024]{2,1,0:T(8,128)(2,1)} broadcast(bf16[]{:T(256)} %constant.64.clone.1), dimensions={} | broadcast | bytes 4194306 | tf_op jit(solution)/shard_map/broadcast_in_dim | solution.py:139
  90.1 1.6 constant_dynamic-update-slice_fusion.1
  91.7 3.1 %constant_dynamic-update-slice_fusion = bf16[32,64,1024]{2,1,0:T(8,128)(2,1)} fusion(bf16[32,64,1024]{2,1,0:T(8,128)(2,1)} %constant_dynamic-update-slice_fusion.1, bf16[16,64,1024]{2,1,0:T(8,128)(2,1)} %collective-permute-done.10, s32[]{:T(128)S(6)} %select_n.65), kind=kLoop, calls=%fused_computation.7 | loop fusion | bytes 4194308 | tf_op jit(solution)/shard_map/dynamic_update_slice | solution.py:141
  94.8 6.3 %copy.7 = bf16[4,512,1024]{1,2,0:T(8,128)(2,1)} copy(bf16[4,512,1024]{2,1,0:T(8,128)(2,1)} %bitcast.5) | data formatting | bytes 8388608 | tf_op jit(solution)/shard_map/reshape | solution.py:142
  101.1 22.6 %all-gather.3.cloned.1.call-done = bf16[16384,256]{1,0:T(8,128)(2,1)} async-done(((bf16[1024,256]{1,0:T(8,128)(2,1)}), bf16[16384,256]{1,0:T(8,128)(2,1)}) %all-gather.3.cloned.1.call-update) | async-done | bytes 8388624 | tf_op jit(solution)/shard_map/all_gather | solution.py:122
  123.7 8.8 %shard_map.68 = (bf16[1024,512]{1,0:T(8,128)(2,1)}, f32[16,8,128]{2,1,0:T(8,128)}) custom-call(s32[1]{0:T(128)} %bitcast.z_ref, bf16[1024,512]{1,0:T(8,128)(2,1)} %base_hbm.1, bf16[4,1024,512]{2,1,0:T(8,128)(2,1)} %bitcast.14, bf16[16,1024,256]{2,1,0:T(8,128)(2,1)} %bitcast.15), custom_call_target="tpu_custom_call" | custom-call | flops 4294967296 | bytes 14680064 | tf_op jit(solution)/shard_map/pallas_call | solution.py:90
  132.5 9.7 %all-to-all-start = ((f32[16,8,128]{2,1,0:T(8,128)}), f32[16,8,128]{2,1,0:T(8,128)S(1)}, u32[]{:S(2)}, u32[]{:S(2)}) async-start(f32[16,8,128]{2,1,0:T(8,128)} %get-tuple-element.5), calls=%async_computation | async-start | bytes 131072 | tf_op jit(solution)/shard_map/all_to_all | solution.py:145
  142.2 13.0 %all-to-all-done = f32[16,8,128]{2,1,0:T(8,128)S(1)} async-done(((f32[16,8,128]{2,1,0:T(8,128)}), f32[16,8,128]{2,1,0:T(8,128)S(1)}, u32[]{:S(2)}, u32[]{:S(2)}) %all-to-all-start) | async-done | bytes 65568 | tf_op jit(solution)/shard_map/all_to_all | solution.py:145
  155.2 2.5 %multiply_convert_fusion = bf16[1024,512]{1,0:T(8,128)(2,1)} fusion(bf16[1024,512]{1,0:T(8,128)(2,1)} %get-tuple-element.4, f32[512]{0:T(512)S(1)} %convert_element_type.18, f32[1024]{0:T(1024)S(1)} %rsqrt_bitcast_fusion), kind=kLoop, calls=%fused_computation | loop fusion | flops 2097152 | bytes 2103296 | tf_op jit(solution)/shard_map/convert_element_type | solution.py:149
  (20 shorter events, 0.3 us)
Async XLA Ops:
  7.2 116.5 %all-gather.3.cloned.1.call-start = ((), (), s32[]{:S(2)}) async-start(), calls=%async_computation.1 | async-start | bytes 8912896 | tf_op jit(solution)/shard_map/all_gather | solution.py:122
  9.6 10.8 %collective-permute-start = (bf16[64,1024]{1,0:T(8,128)(2,1)S(1)}, bf16[64,1024]{1,0:T(8,128)(2,1)S(1)}, u32[]{:S(2)}, u32[]{:S(2)}) collective-permute-start(bf16[64,1024]{1,0:T(8,128)(2,1)S(1)} %get-tuple-element.6), channel_id=1, source_target_pairs={{0,0},{4,84},{8,24},{12,76},{16,128},{20,212},{24,152},{28,204},{3... | collective-permute-start | bytes 393224 | tf_op jit(solution)/shard_map/ppermute | solution.py:125
  20.4 0.7 collective-permute-start.1
  21.1 0.7 collective-permute-start.2
  21.8 9.3 %collective-permute-start.3 = (bf16[64,1024]{1,0:T(8,128)(2,1)S(1)}, bf16[64,1024]{1,0:T(8,128)(2,1)S(1)}, u32[]{:S(2)}, u32[]{:S(2)}) collective-permute-start(bf16[64,1024]{1,0:T(8,128)(2,1)S(1)} %collective-permute-done.2), channel_id=1, source_target_pairs={{0,128},{16,144},{32,160},{48,176},{64,192},{80,208},{96,224},{112... | collective-permute-start | bytes 393224 | tf_op jit(solution)/shard_map/ppermute | solution.py:129
  25.1 8.5 %collective-permute-start.4 = (bf16[64,1024]{1,0:T(8,128)(2,1)S(1)}, bf16[64,1024]{1,0:T(8,128)(2,1)S(1)}, u32[]{:S(2)}, u32[]{:S(2)}) collective-permute-start(bf16[64,1024]{1,0:T(8,128)(2,1)S(1)} %collective-permute-done.2), channel_id=1, source_target_pairs={{0,256},{16,272},{32,288},{48,304},{64,320},{80,336},{96,352},{112... | collective-permute-start | bytes 393224 | tf_op jit(solution)/shard_map/ppermute | solution.py:129
  27.0 7.8 %collective-permute-start.5 = (bf16[64,1024]{1,0:T(8,128)(2,1)S(1)}, bf16[64,1024]{1,0:T(8,128)(2,1)S(1)}, u32[]{:S(2)}, u32[]{:S(2)}) collective-permute-start(bf16[64,1024]{1,0:T(8,128)(2,1)S(1)} %collective-permute-done.2), channel_id=1, source_target_pairs={{0,384},{16,400},{32,416},{48,432},{64,448},{80,464},{96,480},{112... | collective-permute-start | bytes 393224 | tf_op jit(solution)/shard_map/ppermute | solution.py:129
  34.8 26.5 %collective-permute-start.7 = (bf16[4,64,1024]{2,1,0:T(8,128)(2,1)S(1)}, bf16[4,64,1024]{2,1,0:T(8,128)(2,1)S(1)}, u32[]{:S(2)}, u32[]{:S(2)}) collective-permute-start(bf16[4,64,1024]{2,1,0:T(8,128)(2,1)S(1)} %bitcast_dynamic-update-slice_fusion), channel_id=1, source_target_pairs={{0,96},{16,112},{32,64},{48,80},{64,32},{80,48},{96,0},{112,16},{1... | collective-permute-start | bytes 1572872 | tf_op jit(solution)/shard_map/ppermute | solution.py:132
  54.2 11.2 %collective-permute-start.6 = (bf16[4,64,1024]{2,1,0:T(8,128)(2,1)S(1)}, bf16[4,64,1024]{2,1,0:T(8,128)(2,1)}, u32[]{:S(2)}, u32[]{:S(2)}) collective-permute-start(bf16[4,64,1024]{2,1,0:T(8,128)(2,1)S(1)} %bitcast_dynamic-update-slice_fusion), channel_id=1, source_target_pairs={{0,32},{16,48},{32,0},{48,16},{64,96},{80,112},{96,64},{112,80},{1... | collective-permute-start | bytes 1572872 | tf_op jit(solution)/shard_map/ppermute | solution.py:131
  61.3 9.5 %collective-permute-start.8 = (bf16[2,64,1024]{2,1,0:T(8,128)(2,1)S(1)}, bf16[2,64,1024]{2,1,0:T(8,128)(2,1)S(1)}, u32[]{:S(2)}, u32[]{:S(2)}) collective-permute-start(bf16[2,64,1024]{2,1,0:T(8,128)(2,1)S(1)} %slice.8), channel_id=1, source_target_pairs={{0,32},{16,48},{32,0},{48,16},{64,96},{80,112},{96,64},{112,80},{1... | collective-permute-start | bytes 786440 | tf_op jit(solution)/shard_map/ppermute | solution.py:133
  66.3 9.7 %collective-permute-start.9 = (bf16[2,64,1024]{2,1,0:T(8,128)(2,1)S(1)}, bf16[2,64,1024]{2,1,0:T(8,128)(2,1)S(1)}, u32[]{:S(2)}, u32[]{:S(2)}) collective-permute-start(bf16[2,64,1024]{2,1,0:T(8,128)(2,1)S(1)} %slice.9), channel_id=1, source_target_pairs={{0,96},{16,112},{32,64},{48,80},{64,32},{80,48},{96,0},{112,16},{1... | collective-permute-start | bytes 786440 | tf_op jit(solution)/shard_map/ppermute | solution.py:134
  76.1 15.6 %collective-permute-start.10 = (bf16[16,64,1024]{2,1,0:T(8,128)(2,1)S(1)}, bf16[16,64,1024]{2,1,0:T(8,128)(2,1)}, u32[]{:S(2)}, u32[]{:S(2)}) collective-permute-start(bf16[16,64,1024]{2,1,0:T(8,128)(2,1)S(1)} %constant_dynamic-update-slice_fusion.2), channel_id=1, source_target_pairs={{0,16},{16,0},{32,48},{48,32},{64,80},{80,64},{96,112},{112,96},{1... | collective-permute-start | bytes 6291464 | tf_op jit(solution)/shard_map/ppermute | solution.py:138
  123.7 18.5 %copy-start = (bf16[512]{0:T(512)(128)(2,1)S(1)}, bf16[512]{0:T(512)(128)(2,1)}, u32[]{:S(2)}) copy-start(bf16[512]{0:T(512)(128)(2,1)} %param.9) | copy-start | bytes 3076
  132.5 22.7 %all-to-all-start = ((f32[16,8,128]{2,1,0:T(8,128)}), f32[16,8,128]{2,1,0:T(8,128)S(1)}, u32[]{:S(2)}, u32[]{:S(2)}) async-start(f32[16,8,128]{2,1,0:T(8,128)} %get-tuple-element.5), calls=%async_computation | async-start | bytes 131072 | tf_op jit(solution)/shard_map/all_to_all | solution.py:145
Sparse Core Ops, SparseCore 0:
  10.1 113.5 all-gather.2

commit v5 on v4

--- a/solution.py
+++ b/solution.py
@@ -54,26 +54,36 @@
     first = z_ref[0] // 4 + z_ref[0] % 4
     copies = []
     for turn in range(4):
-        plane = pl.ds((first - turn + 4) % 4 * 4, 4)
-        copies.append(
-            (
-                pltpu.make_async_copy(weight_hbm.at[turn], weight.at[turn], sems.at[2 * turn]),
-                pltpu.make_async_copy(
-                    context_hbm.at[plane], context.at[turn], sems.at[2 * turn + 1]
-                ),
+        for half in range(2):
+            plane = pl.ds((first - turn + 4) % 4 * 4 + 2 * half, 2)
+            rows = pl.ds(512 * half, 512)
+            k = 4 * turn + 2 * half
+            copies.append(
+                (
+                    pltpu.make_async_copy(
+                        weight_hbm.at[turn, rows], weight.at[turn, rows], sems.at[k]
+                    ),
+                    pltpu.make_async_copy(
+                        context_hbm.at[plane], context.at[turn, pl.ds(2 * half, 2)], sems.at[k + 1]
+                    ),
+                )
             )
-        )
-    base_copy = pltpu.make_async_copy(base_hbm, base, sems.at[8])
+    base_copy = pltpu.make_async_copy(base_hbm, base, sems.at[16])
     for pair in copies:
         pair[0].start()
         pair[1].start()
     base_copy.start()
     total = 0
-    for turn, pair in enumerate(copies):
+    for chunk, pair in enumerate(copies):
+        turn, half = chunk // 2, chunk % 2
         pair[0].wait()
         pair[1].wait()
-        block = jnp.concatenate([context[turn, i] for i in range(4)], axis=1)
-        total += jnp.dot(block, weight[turn], preferred_element_type=jnp.float32)
+        block = jnp.concatenate([context[turn, 2 * half + i] for i in range(2)], axis=1)
+        total += jnp.dot(
+            block,
+            weight[turn, 512 * half : 512 * (half + 1)],
+            preferred_element_type=jnp.float32,
+        )
     base_copy.wait()
     total += base[...].astype(jnp.float32)
     out_ref[...] = total.astype(jnp.bfloat16)
@@ -100,9 +110,9 @@
             pltpu.VMEM((TOK, COLS), jnp.bfloat16),
             pltpu.VMEM((4, 1024, COLS), jnp.bfloat16),
             pltpu.VMEM((4, 4, TOK, FEAT), jnp.bfloat16),
-            pltpu.SemaphoreType.DMA((9,)),
+            pltpu.SemaphoreType.DMA((17,)),
         ],
-        compiler_params=pltpu.CompilerParams(vmem_limit_bytes=60 * 1024 * 1024),
+        compiler_params=pltpu.CompilerParams(vmem_limit_bytes=50 * 1024 * 1024),
         cost_estimate=pl.CostEstimate(
             flops=2 * TOK * COLS * H,
             bytes_accessed=(TOK + COLS) * H * 2 + TOK * COLS * 4,

time: 165 us -> 163 us (0.988)
  local copies, waits for them, and re-layouts: 16.1 us -> 13.6 us
  waiting for transfers between devices: 59.8 us -> 62.2 us
    ppermute x1, waiting for transfers between devices: 0.01 us -> 3.03 us  [shards(): other = lax.ppermute(plane, 'fsdp', partner(0, 0, 1))]
    broadcast_in_dim x1, local copies, waits for them, and re-layouts: 2.47 us -> 0.52 us  [shards(): pieces = jnp.zeros((32, 64, 1024), jnp.bfloat16)]
    unnamed x2 -> x6, local copies, waits for them, and re-layouts: 0.01 us -> 1.93 us
  transfers between devices with their start and end apart: 13 -> 13, of which waited for: 8 -> 9; matrix products, arithmetic and copies ran while one was open for 11% -> 8% of each run, Pallas kernels for 0% -> 0%
where the time goes in v5:
time: 163 us; the launch traced here: 162 us
  waiting for transfers between devices  62.2 us (38%)
  starting transfers between devices  61.2 us (38%)
  between operations  14.4 us (9%)
  local copies, waits for them, and re-layouts  13.6 us (8%)
  Pallas kernels  7.81 us (5%)
  other arithmetic  3.04 us (2%)
    all_gather x1, waiting for transfers between devices, shards(): gathered = lax.all_gather(context, Z, axis=0)  21.9 us
    ppermute x1, starting transfers between devices, shards(): back = lax.ppermute(row, 'fsdp', partner(0, 3, 0))  19.3 us
    all_to_all x1, waiting for transfers between devices, shards(): totals = jnp.sum(lax.all_to_all(squares, Z, 0, 0, tiled=True), axis=0)  13 us
    ppermute x1, starting transfers between devices, shards(): other = lax.ppermute(plane, 'fsdp', partner(0, 0, 1))  11.5 us
    all_to_all x1, starting transfers between devices, shards(): totals = jnp.sum(lax.all_to_all(squares, Z, 0, 0, tiled=True), axis=0)  9.66 us
    ppermute x3, starting transfers between devices, shards(): got = piece if dx == 0 else lax.ppermute(piece, 'fsdp', partner(dx, 0, 0))  9.21 us
    ppermute x3, waiting for transfers between devices, shards(): piece = lax.ppermute(piece, ALL, pairs)  8.85 us
    pallas_call x1, Pallas kernels, product(): pl.pallas_call(kernel, out_shape=[jax.ShapeDtypeStruct((TOK, COLS), jnp.b...  7.81 us
  transfers between devices with their start and end apart: 13, of which 9 were waited for; matrix products, arithmetic and copies ran while one was open for 8% of the time, Pallas kernels for 0%

profile of v5, /device:TPU:12, one launch (start us, length us, event | category | flops | bytes accessed | tf_op | source)
XLA Modules:
  0.0 162.3 jit_solution(2676799292725508397)
XLA Ops:
  7.2 0.7 all-gather.3.cloned.1.call-update
  7.9 1.7 %fusion = (bf16[64,1024]{1,0:T(8,128)(2,1)S(1)}, f32[64,1024]{1,0:T(8,128)}) fusion(f32[64,1024]{1,0:T(8,128)} %param.8, bf16[64,1024]{1,0:T(8,128)(2,1)} %param.7), kind=kLoop, calls=%fused_computation.14 | loop fusion | flops 327680 | bytes 786432 | tf_op jit(solution)/shard_map/convert_element_type | solution.py:126
  9.6 1.9 %collective-permute-start = (bf16[64,1024]{1,0:T(8,128)(2,1)S(1)}, bf16[64,1024]{1,0:T(8,128)(2,1)S(1)}, u32[]{:S(2)}, u32[]{:S(2)}) collective-permute-start(bf16[64,1024]{1,0:T(8,128)(2,1)S(1)} %get-tuple-element.6), channel_id=1, source_target_pairs={{0,0},{4,84},{8,24},{12,76},{16,128},{20,212},{24,152},{28,204},{3... | collective-permute-start | bytes 393224 | tf_op jit(solution)/shard_map/ppermute | solution.py:135
  11.5 8.8 %collective-permute-done = bf16[64,1024]{1,0:T(8,128)(2,1)S(1)} collective-permute-done((bf16[64,1024]{1,0:T(8,128)(2,1)S(1)}, bf16[64,1024]{1,0:T(8,128)(2,1)S(1)}, u32[]{:S(2)}, u32[]{:S(2)}) %collective-permute-start) | collective-permute-done | bytes 131104 | tf_op jit(solution)/shard_map/ppermute | solution.py:135
  20.4 0.7 collective-permute-start.1
  21.1 0.7 collective-permute-start.2
  21.8 3.3 %collective-permute-start.3 = (bf16[64,1024]{1,0:T(8,128)(2,1)S(1)}, bf16[64,1024]{1,0:T(8,128)(2,1)S(1)}, u32[]{:S(2)}, u32[]{:S(2)}) collective-permute-start(bf16[64,1024]{1,0:T(8,128)(2,1)S(1)} %collective-permute-done.2), channel_id=1, source_target_pairs={{0,128},{16,144},{32,160},{48,176},{64,192},{80,208},{96,224},{112... | collective-permute-start | bytes 393224 | tf_op jit(solution)/shard_map/ppermute | solution.py:139
  25.1 1.9 %collective-permute-start.4 = (bf16[64,1024]{1,0:T(8,128)(2,1)S(1)}, bf16[64,1024]{1,0:T(8,128)(2,1)S(1)}, u32[]{:S(2)}, u32[]{:S(2)}) collective-permute-start(bf16[64,1024]{1,0:T(8,128)(2,1)S(1)} %collective-permute-done.2), channel_id=1, source_target_pairs={{0,256},{16,272},{32,288},{48,304},{64,320},{80,336},{96,352},{112... | collective-permute-start | bytes 393224 | tf_op jit(solution)/shard_map/ppermute | solution.py:139
  27.0 4.0 %collective-permute-start.5 = (bf16[64,1024]{1,0:T(8,128)(2,1)S(1)}, bf16[64,1024]{1,0:T(8,128)(2,1)S(1)}, u32[]{:S(2)}, u32[]{:S(2)}) collective-permute-start(bf16[64,1024]{1,0:T(8,128)(2,1)S(1)} %collective-permute-done.2), channel_id=1, source_target_pairs={{0,384},{16,400},{32,416},{48,432},{64,448},{80,464},{96,480},{112... | collective-permute-start | bytes 393224 | tf_op jit(solution)/shard_map/ppermute | solution.py:139
  31.1 2.4 %collective-permute-done.4 = bf16[64,1024]{1,0:T(8,128)(2,1)S(1)} collective-permute-done((bf16[64,1024]{1,0:T(8,128)(2,1)S(1)}, bf16[64,1024]{1,0:T(8,128)(2,1)S(1)}, u32[]{:S(2)}, u32[]{:S(2)}) %collective-permute-start.4) | collective-permute-done | bytes 131104 | tf_op jit(solution)/shard_map/ppermute | solution.py:139
  33.5 1.3 collective-permute-done.5
  34.8 19.3 %collective-permute-start.7 = (bf16[4,64,1024]{2,1,0:T(8,128)(2,1)S(1)}, bf16[4,64,1024]{2,1,0:T(8,128)(2,1)S(1)}, u32[]{:S(2)}, u32[]{:S(2)}) collective-permute-start(bf16[4,64,1024]{2,1,0:T(8,128)(2,1)S(1)} %bitcast_dynamic-update-slice_fusion), channel_id=1, source_target_pairs={{0,96},{16,112},{32,64},{48,80},{64,32},{80,48},{96,0},{112,16},{1... | collective-permute-start | bytes 1572872 | tf_op jit(solution)/shard_map/ppermute | solution.py:142
  54.2 2.5 %collective-permute-start.6 = (bf16[4,64,1024]{2,1,0:T(8,128)(2,1)S(1)}, bf16[4,64,1024]{2,1,0:T(8,128)(2,1)}, u32[]{:S(2)}, u32[]{:S(2)}) collective-permute-start(bf16[4,64,1024]{2,1,0:T(8,128)(2,1)S(1)} %bitcast_dynamic-update-slice_fusion), channel_id=1, source_target_pairs={{0,32},{16,48},{32,0},{48,16},{64,96},{80,112},{96,64},{112,80},{1... | collective-permute-start | bytes 1572872 | tf_op jit(solution)/shard_map/ppermute | solution.py:141
  56.7 4.6 %collective-permute-done.7 = bf16[4,64,1024]{2,1,0:T(8,128)(2,1)S(1)} collective-permute-done((bf16[4,64,1024]{2,1,0:T(8,128)(2,1)S(1)}, bf16[4,64,1024]{2,1,0:T(8,128)(2,1)S(1)}, u32[]{:S(2)}, u32[]{:S(2)}) %collective-permute-start.7) | collective-permute-done | bytes 524320 | tf_op jit(solution)/shard_map/ppermute | solution.py:142
  61.3 2.5 %collective-permute-start.8 = (bf16[2,64,1024]{2,1,0:T(8,128)(2,1)S(1)}, bf16[2,64,1024]{2,1,0:T(8,128)(2,1)S(1)}, u32[]{:S(2)}, u32[]{:S(2)}) collective-permute-start(bf16[2,64,1024]{2,1,0:T(8,128)(2,1)S(1)} %slice.8), channel_id=1, source_target_pairs={{0,32},{16,48},{32,0},{48,16},{64,96},{80,112},{96,64},{112,80},{1... | collective-permute-start | bytes 786440 | tf_op jit(solution)/shard_map/ppermute | solution.py:143
  64.1 1.2 collective-permute-done.6
  65.4 1.0 slice.9
  66.3 3.3 %collective-permute-start.9 = (bf16[2,64,1024]{2,1,0:T(8,128)(2,1)S(1)}, bf16[2,64,1024]{2,1,0:T(8,128)(2,1)S(1)}, u32[]{:S(2)}, u32[]{:S(2)}) collective-permute-start(bf16[2,64,1024]{2,1,0:T(8,128)(2,1)S(1)} %slice.9), channel_id=1, source_target_pairs={{0,96},{16,112},{32,64},{48,80},{64,32},{80,48},{96,0},{112,16},{1... | collective-permute-start | bytes 786440 | tf_op jit(solution)/shard_map/ppermute | solution.py:144
  69.6 1.1 constant_dynamic-update-slice_fusion.5
  70.8 5.2 %collective-permute-done.9 = bf16[2,64,1024]{2,1,0:T(8,128)(2,1)S(1)} collective-permute-done((bf16[2,64,1024]{2,1,0:T(8,128)(2,1)S(1)}, bf16[2,64,1024]{2,1,0:T(8,128)(2,1)S(1)}, u32[]{:S(2)}, u32[]{:S(2)}) %collective-permute-start.9) | collective-permute-done | bytes 262176 | tf_op jit(solution)/shard_map/ppermute | solution.py:144
  76.1 11.5 %collective-permute-start.10 = (bf16[16,64,1024]{2,1,0:T(8,128)(2,1)S(1)}, bf16[16,64,1024]{2,1,0:T(8,128)(2,1)}, u32[]{:S(2)}, u32[]{:S(2)}) collective-permute-start(bf16[16,64,1024]{2,1,0:T(8,128)(2,1)S(1)} %constant_dynamic-update-slice_fusion.2), channel_id=1, source_target_pairs={{0,16},{16,0},{32,48},{48,32},{64,80},{80,64},{96,112},{112,96},{1... | collective-permute-start | bytes 6291464 | tf_op jit(solution)/shard_map/ppermute | solution.py:148
  87.6 0.5 broadcast_in_dim.27
  88.1 0.3 constant_dynamic-update-slice_fusion.1
  88.4 3.0 %collective-permute-done.10 = bf16[16,64,1024]{2,1,0:T(8,128)(2,1)} collective-permute-done((bf16[16,64,1024]{2,1,0:T(8,128)(2,1)S(1)}, bf16[16,64,1024]{2,1,0:T(8,128)(2,1)}, u32[]{:S(2)}, u32[]{:S(2)}) %collective-permute-start.10) | collective-permute-done | bytes 2097184 | tf_op jit(solution)/shard_map/ppermute | solution.py:148
  91.5 1.9 %constant_dynamic-update-slice_fusion = bf16[32,64,1024]{2,1,0:T(8,128)(2,1)S(1)} fusion(bf16[32,64,1024]{2,1,0:T(8,128)(2,1)S(1)} %constant_dynamic-update-slice_fusion.1, bf16[16,64,1024]{2,1,0:T(8,128)(2,1)} %collective-permute-done.10, s32[]{:T(128)S(6)} %select_n.65), kind=kLoop, calls=%fused_computation.7 | loop fusion | bytes 4194308 | tf_op jit(solution)/shard_map/dynamic_update_slice | solution.py:151
  93.4 1.9 %copy-done.1 = bf16[32,64,1024]{2,1,0:T(8,128)(2,1)} copy-done((bf16[32,64,1024]{2,1,0:T(8,128)(2,1)}, bf16[32,64,1024]{2,1,0:T(8,128)(2,1)S(1)}, u32[]{:S(2)}) %copy-start.1) | copy-done | bytes 4194328
  95.3 6.4 %copy.7 = bf16[4,512,1024]{1,2,0:T(8,128)(2,1)} copy(bf16[4,512,1024]{2,1,0:T(8,128)(2,1)} %bitcast.14) | data formatting | bytes 8388608 | tf_op jit(solution)/shard_map/reshape | solution.py:152
  101.7 21.9 %all-gather.3.cloned.1.call-done = bf16[16384,256]{1,0:T(8,128)(2,1)} async-done(((bf16[1024,256]{1,0:T(8,128)(2,1)}), bf16[16384,256]{1,0:T(8,128)(2,1)}) %all-gather.3.cloned.1.call-update) | async-done | bytes 8388624 | tf_op jit(solution)/shard_map/all_gather | solution.py:132
  123.7 7.8 %shard_map.68 = (bf16[1024,512]{1,0:T(8,128)(2,1)S(1)}, f32[16,8,128]{2,1,0:T(8,128)}) custom-call(s32[1]{0:T(128)} %bitcast.z_ref, bf16[1024,512]{1,0:T(8,128)(2,1)S(1)} %copy-done, bf16[4,1024,512]{2,1,0:T(8,128)(2,1)} %bitcast.15, bf16[16,1024,256]{2,1,0:T(8,128)(2,1)} %bitcast.16), custom_call_target="tpu_custom_call" | custom-call | flops 4294967296 | bytes 14680064 | tf_op jit(solution)/shard_map/pallas_call | solution.py:100
  131.5 9.7 %all-to-all-start = ((f32[16,8,128]{2,1,0:T(8,128)}), f32[16,8,128]{2,1,0:T(8,128)S(1)}, u32[]{:S(2)}, u32[]{:S(2)}) async-start(f32[16,8,128]{2,1,0:T(8,128)} %get-tuple-element.5), calls=%async_computation | async-start | bytes 131072 | tf_op jit(solution)/shard_map/all_to_all | solution.py:155
  141.2 13.0 %all-to-all-done = f32[16,8,128]{2,1,0:T(8,128)S(1)} async-done(((f32[16,8,128]{2,1,0:T(8,128)}), f32[16,8,128]{2,1,0:T(8,128)S(1)}, u32[]{:S(2)}, u32[]{:S(2)}) %all-to-all-start) | async-done | bytes 65568 | tf_op jit(solution)/shard_map/all_to_all | solution.py:155
  154.2 1.3 multiply_convert_fusion
  (24 shorter events, 0.6 us)
Async XLA Ops:
  7.2 116.5 %all-gather.3.cloned.1.call-start = ((), (), s32[]{:S(2)}) async-start(), calls=%async_computation.1 | async-start | bytes 8912896 | tf_op jit(solution)/shard_map/all_gather | solution.py:132
  9.6 10.8 %collective-permute-start = (bf16[64,1024]{1,0:T(8,128)(2,1)S(1)}, bf16[64,1024]{1,0:T(8,128)(2,1)S(1)}, u32[]{:S(2)}, u32[]{:S(2)}) collective-permute-start(bf16[64,1024]{1,0:T(8,128)(2,1)S(1)} %get-tuple-element.6), channel_id=1, source_target_pairs={{0,0},{4,84},{8,24},{12,76},{16,128},{20,212},{24,152},{28,204},{3... | collective-permute-start | bytes 393224 | tf_op jit(solution)/shard_map/ppermute | solution.py:135
  20.4 0.7 collective-permute-start.1
  21.1 0.7 collective-permute-start.2
  21.8 9.3 %collective-permute-start.3 = (bf16[64,1024]{1,0:T(8,128)(2,1)S(1)}, bf16[64,1024]{1,0:T(8,128)(2,1)S(1)}, u32[]{:S(2)}, u32[]{:S(2)}) collective-permute-start(bf16[64,1024]{1,0:T(8,128)(2,1)S(1)} %collective-permute-done.2), channel_id=1, source_target_pairs={{0,128},{16,144},{32,160},{48,176},{64,192},{80,208},{96,224},{112... | collective-permute-start | bytes 393224 | tf_op jit(solution)/shard_map/ppermute | solution.py:139
  25.1 8.5 %collective-permute-start.4 = (bf16[64,1024]{1,0:T(8,128)(2,1)S(1)}, bf16[64,1024]{1,0:T(8,128)(2,1)S(1)}, u32[]{:S(2)}, u32[]{:S(2)}) collective-permute-start(bf16[64,1024]{1,0:T(8,128)(2,1)S(1)} %collective-permute-done.2), channel_id=1, source_target_pairs={{0,256},{16,272},{32,288},{48,304},{64,320},{80,336},{96,352},{112... | collective-permute-start | bytes 393224 | tf_op jit(solution)/shard_map/ppermute | solution.py:139
  27.0 7.8 %collective-permute-start.5 = (bf16[64,1024]{1,0:T(8,128)(2,1)S(1)}, bf16[64,1024]{1,0:T(8,128)(2,1)S(1)}, u32[]{:S(2)}, u32[]{:S(2)}) collective-permute-start(bf16[64,1024]{1,0:T(8,128)(2,1)S(1)} %collective-permute-done.2), channel_id=1, source_target_pairs={{0,384},{16,400},{32,416},{48,432},{64,448},{80,464},{96,480},{112... | collective-permute-start | bytes 393224 | tf_op jit(solution)/shard_map/ppermute | solution.py:139
  34.8 26.5 %collective-permute-start.7 = (bf16[4,64,1024]{2,1,0:T(8,128)(2,1)S(1)}, bf16[4,64,1024]{2,1,0:T(8,128)(2,1)S(1)}, u32[]{:S(2)}, u32[]{:S(2)}) collective-permute-start(bf16[4,64,1024]{2,1,0:T(8,128)(2,1)S(1)} %bitcast_dynamic-update-slice_fusion), channel_id=1, source_target_pairs={{0,96},{16,112},{32,64},{48,80},{64,32},{80,48},{96,0},{112,16},{1... | collective-permute-start | bytes 1572872 | tf_op jit(solution)/shard_map/ppermute | solution.py:142
  54.2 11.2 %collective-permute-start.6 = (bf16[4,64,1024]{2,1,0:T(8,128)(2,1)S(1)}, bf16[4,64,1024]{2,1,0:T(8,128)(2,1)}, u32[]{:S(2)}, u32[]{:S(2)}) collective-permute-start(bf16[4,64,1024]{2,1,0:T(8,128)(2,1)S(1)} %bitcast_dynamic-update-slice_fusion), channel_id=1, source_target_pairs={{0,32},{16,48},{32,0},{48,16},{64,96},{80,112},{96,64},{112,80},{1... | collective-permute-start | bytes 1572872 | tf_op jit(solution)/shard_map/ppermute | solution.py:141
  61.3 9.5 %collective-permute-start.8 = (bf16[2,64,1024]{2,1,0:T(8,128)(2,1)S(1)}, bf16[2,64,1024]{2,1,0:T(8,128)(2,1)S(1)}, u32[]{:S(2)}, u32[]{:S(2)}) collective-permute-start(bf16[2,64,1024]{2,1,0:T(8,128)(2,1)S(1)} %slice.8), channel_id=1, source_target_pairs={{0,32},{16,48},{32,0},{48,16},{64,96},{80,112},{96,64},{112,80},{1... | collective-permute-start | bytes 786440 | tf_op jit(solution)/shard_map/ppermute | solution.py:143
  66.3 9.7 %collective-permute-start.9 = (bf16[2,64,1024]{2,1,0:T(8,128)(2,1)S(1)}, bf16[2,64,1024]{2,1,0:T(8,128)(2,1)S(1)}, u32[]{:S(2)}, u32[]{:S(2)}) collective-permute-start(bf16[2,64,1024]{2,1,0:T(8,128)(2,1)S(1)} %slice.9), channel_id=1, source_target_pairs={{0,96},{16,112},{32,64},{48,80},{64,32},{80,48},{96,0},{112,16},{1... | collective-permute-start | bytes 786440 | tf_op jit(solution)/shard_map/ppermute | solution.py:144
  76.1 15.4 %collective-permute-start.10 = (bf16[16,64,1024]{2,1,0:T(8,128)(2,1)S(1)}, bf16[16,64,1024]{2,1,0:T(8,128)(2,1)}, u32[]{:S(2)}, u32[]{:S(2)}) collective-permute-start(bf16[16,64,1024]{2,1,0:T(8,128)(2,1)S(1)} %constant_dynamic-update-slice_fusion.2), channel_id=1, source_target_pairs={{0,16},{16,0},{32,48},{48,32},{64,80},{80,64},{96,112},{112,96},{1... | collective-permute-start | bytes 6291464 | tf_op jit(solution)/shard_map/ppermute | solution.py:148
  93.4 1.9 %copy-start.1 = (bf16[32,64,1024]{2,1,0:T(8,128)(2,1)}, bf16[32,64,1024]{2,1,0:T(8,128)(2,1)S(1)}, u32[]{:S(2)}) copy-start(bf16[32,64,1024]{2,1,0:T(8,128)(2,1)S(1)} %constant_dynamic-update-slice_fusion) | copy-start | bytes 12582916
  95.3 28.3 %copy-start = (bf16[1024,512]{1,0:T(8,128)(2,1)S(1)}, bf16[1024,512]{1,0:T(8,128)(2,1)}, u32[]{:S(2)}) copy-start(bf16[1024,512]{1,0:T(8,128)(2,1)} %base_hbm.1) | copy-start | bytes 3145732
  123.7 17.5 %copy-start.2 = (bf16[512]{0:T(512)(128)(2,1)S(1)}, bf16[512]{0:T(512)(128)(2,1)}, u32[]{:S(2)}) copy-start(bf16[512]{0:T(512)(128)(2,1)} %param.9) | copy-start | bytes 3076
  131.5 22.7 %all-to-all-start = ((f32[16,8,128]{2,1,0:T(8,128)}), f32[16,8,128]{2,1,0:T(8,128)S(1)}, u32[]{:S(2)}, u32[]{:S(2)}) async-start(f32[16,8,128]{2,1,0:T(8,128)} %get-tuple-element.5), calls=%async_computation | async-start | bytes 131072 | tf_op jit(solution)/shard_map/all_to_all | solution.py:155
Sparse Core Ops, SparseCore 0:
  10.1 113.5 all-gather.2

commit v6 on v5

--- a/solution.py
+++ b/solution.py
@@ -50,7 +50,7 @@
     return pairs
 
 
-def kernel(z_ref, base_hbm, weight_hbm, context_hbm, out_ref, squares_ref, base, weight, context, sems):
+def kernel(z_ref, base, weight_hbm, context_hbm, out_ref, squares_ref, weight, context, sems):
     first = z_ref[0] // 4 + z_ref[0] % 4
     copies = []
     for turn in range(4):
@@ -68,11 +68,9 @@
                     ),
                 )
             )
-    base_copy = pltpu.make_async_copy(base_hbm, base, sems.at[16])
     for pair in copies:
         pair[0].start()
         pair[1].start()
-    base_copy.start()
     total = 0
     for chunk, pair in enumerate(copies):
         turn, half = chunk // 2, chunk % 2
@@ -84,7 +82,6 @@
             weight[turn, 512 * half : 512 * (half + 1)],
             preferred_element_type=jnp.float32,
         )
-    base_copy.wait()
     total += base[...].astype(jnp.float32)
     out_ref[...] = total.astype(jnp.bfloat16)
     squared = total * total
@@ -104,13 +101,13 @@
             jax.ShapeDtypeStruct((NZ, TOK // 128, 128), jnp.float32),
         ],
         in_specs=[pl.BlockSpec(memory_space=pltpu.SMEM)]
-        + [pl.BlockSpec(memory_space=pltpu.HBM)] * 3,
+        + [pl.BlockSpec(memory_space=pltpu.VMEM)]
+        + [pl.BlockSpec(memory_space=pltpu.HBM)] * 2,
         out_specs=[pl.BlockSpec(memory_space=pltpu.VMEM)] * 2,
         scratch_shapes=[
-            pltpu.VMEM((TOK, COLS), jnp.bfloat16),
             pltpu.VMEM((4, 1024, COLS), jnp.bfloat16),
             pltpu.VMEM((4, 4, TOK, FEAT), jnp.bfloat16),
-            pltpu.SemaphoreType.DMA((17,)),
+            pltpu.SemaphoreType.DMA((16,)),
         ],
         compiler_params=pltpu.CompilerParams(vmem_limit_bytes=50 * 1024 * 1024),
         cost_estimate=pl.CostEstimate(

time: 163 us -> 163 us (level)
  no operation moved by 1% of the time
where the time goes in v6:
time: 163 us; the launch traced here: 162 us
  waiting for transfers between devices  62.2 us (38%)
  starting transfers between devices  61.2 us (38%)
  between operations  14.4 us (9%)
  local copies, waits for them, and re-layouts  13.6 us (8%)
  Pallas kernels  7.55 us (5%)
  other arithmetic  3.04 us (2%)
    all_gather x1, waiting for transfers between devices, shards(): gathered = lax.all_gather(context, Z, axis=0)  21.9 us
    ppermute x1, starting transfers between devices, shards(): back = lax.ppermute(row, 'fsdp', partner(0, 3, 0))  19.3 us
    all_to_all x1, waiting for transfers between devices, shards(): totals = jnp.sum(lax.all_to_all(squares, Z, 0, 0, tiled=True), axis=0)  13 us
    ppermute x1, starting transfers between devices, shards(): other = lax.ppermute(plane, 'fsdp', partner(0, 0, 1))  11.5 us
    all_to_all x1, starting transfers between devices, shards(): totals = jnp.sum(lax.all_to_all(squares, Z, 0, 0, tiled=True), axis=0)  9.66 us
    ppermute x3, starting transfers between devices, shards(): got = piece if dx == 0 else lax.ppermute(piece, 'fsdp', partner(dx, 0, 0))  9.21 us
    ppermute x3, waiting for transfers between devices, shards(): piece = lax.ppermute(piece, ALL, pairs)  8.85 us
    pallas_call x1, Pallas kernels, product(): pl.pallas_call(kernel, out_shape=[jax.ShapeDtypeStruct((TOK, COLS), jnp.b...  7.55 us
  transfers between devices with their start and end apart: 13, of which 9 were waited for; matrix products, arithmetic and copies ran while one was open for 8% of the time, Pallas kernels for 0%

profile of v6, /device:TPU:12, one launch (start us, length us, event | category | flops | bytes accessed | tf_op | source)
XLA Modules:
  0.0 162.1 jit_solution(1328632928826295270)
XLA Ops:
  7.2 0.7 all-gather.3.cloned.1.call-update
  7.9 1.7 %fusion = (bf16[64,1024]{1,0:T(8,128)(2,1)S(1)}, f32[64,1024]{1,0:T(8,128)}) fusion(f32[64,1024]{1,0:T(8,128)} %param.8, bf16[64,1024]{1,0:T(8,128)(2,1)} %param.7), kind=kLoop, calls=%fused_computation.14 | loop fusion | flops 327680 | bytes 786432 | tf_op jit(solution)/shard_map/convert_element_type | solution.py:123
  9.6 1.9 %collective-permute-start = (bf16[64,1024]{1,0:T(8,128)(2,1)S(1)}, bf16[64,1024]{1,0:T(8,128)(2,1)S(1)}, u32[]{:S(2)}, u32[]{:S(2)}) collective-permute-start(bf16[64,1024]{1,0:T(8,128)(2,1)S(1)} %get-tuple-element.6), channel_id=1, source_target_pairs={{0,0},{4,84},{8,24},{12,76},{16,128},{20,212},{24,152},{28,204},{3... | collective-permute-start | bytes 393224 | tf_op jit(solution)/shard_map/ppermute | solution.py:132
  11.5 8.8 %collective-permute-done = bf16[64,1024]{1,0:T(8,128)(2,1)S(1)} collective-permute-done((bf16[64,1024]{1,0:T(8,128)(2,1)S(1)}, bf16[64,1024]{1,0:T(8,128)(2,1)S(1)}, u32[]{:S(2)}, u32[]{:S(2)}) %collective-permute-start) | collective-permute-done | bytes 131104 | tf_op jit(solution)/shard_map/ppermute | solution.py:132
  20.4 0.7 collective-permute-start.1
  21.1 0.7 collective-permute-start.2
  21.8 3.3 %collective-permute-start.3 = (bf16[64,1024]{1,0:T(8,128)(2,1)S(1)}, bf16[64,1024]{1,0:T(8,128)(2,1)S(1)}, u32[]{:S(2)}, u32[]{:S(2)}) collective-permute-start(bf16[64,1024]{1,0:T(8,128)(2,1)S(1)} %collective-permute-done.2), channel_id=1, source_target_pairs={{0,128},{16,144},{32,160},{48,176},{64,192},{80,208},{96,224},{112... | collective-permute-start | bytes 393224 | tf_op jit(solution)/shard_map/ppermute | solution.py:136
  25.1 1.9 %collective-permute-start.4 = (bf16[64,1024]{1,0:T(8,128)(2,1)S(1)}, bf16[64,1024]{1,0:T(8,128)(2,1)S(1)}, u32[]{:S(2)}, u32[]{:S(2)}) collective-permute-start(bf16[64,1024]{1,0:T(8,128)(2,1)S(1)} %collective-permute-done.2), channel_id=1, source_target_pairs={{0,256},{16,272},{32,288},{48,304},{64,320},{80,336},{96,352},{112... | collective-permute-start | bytes 393224 | tf_op jit(solution)/shard_map/ppermute | solution.py:136
  27.0 4.0 %collective-permute-start.5 = (bf16[64,1024]{1,0:T(8,128)(2,1)S(1)}, bf16[64,1024]{1,0:T(8,128)(2,1)S(1)}, u32[]{:S(2)}, u32[]{:S(2)}) collective-permute-start(bf16[64,1024]{1,0:T(8,128)(2,1)S(1)} %collective-permute-done.2), channel_id=1, source_target_pairs={{0,384},{16,400},{32,416},{48,432},{64,448},{80,464},{96,480},{112... | collective-permute-start | bytes 393224 | tf_op jit(solution)/shard_map/ppermute | solution.py:136
  31.1 2.4 %collective-permute-done.4 = bf16[64,1024]{1,0:T(8,128)(2,1)S(1)} collective-permute-done((bf16[64,1024]{1,0:T(8,128)(2,1)S(1)}, bf16[64,1024]{1,0:T(8,128)(2,1)S(1)}, u32[]{:S(2)}, u32[]{:S(2)}) %collective-permute-start.4) | collective-permute-done | bytes 131104 | tf_op jit(solution)/shard_map/ppermute | solution.py:136
  33.5 1.3 collective-permute-done.5
  34.8 19.3 %collective-permute-start.7 = (bf16[4,64,1024]{2,1,0:T(8,128)(2,1)S(1)}, bf16[4,64,1024]{2,1,0:T(8,128)(2,1)S(1)}, u32[]{:S(2)}, u32[]{:S(2)}) collective-permute-start(bf16[4,64,1024]{2,1,0:T(8,128)(2,1)S(1)} %bitcast_dynamic-update-slice_fusion), channel_id=1, source_target_pairs={{0,96},{16,112},{32,64},{48,80},{64,32},{80,48},{96,0},{112,16},{1... | collective-permute-start | bytes 1572872 | tf_op jit(solution)/shard_map/ppermute | solution.py:139
  54.2 2.5 %collective-permute-start.6 = (bf16[4,64,1024]{2,1,0:T(8,128)(2,1)S(1)}, bf16[4,64,1024]{2,1,0:T(8,128)(2,1)}, u32[]{:S(2)}, u32[]{:S(2)}) collective-permute-start(bf16[4,64,1024]{2,1,0:T(8,128)(2,1)S(1)} %bitcast_dynamic-update-slice_fusion), channel_id=1, source_target_pairs={{0,32},{16,48},{32,0},{48,16},{64,96},{80,112},{96,64},{112,80},{1... | collective-permute-start | bytes 1572872 | tf_op jit(solution)/shard_map/ppermute | solution.py:138
  56.7 4.6 %collective-permute-done.7 = bf16[4,64,1024]{2,1,0:T(8,128)(2,1)S(1)} collective-permute-done((bf16[4,64,1024]{2,1,0:T(8,128)(2,1)S(1)}, bf16[4,64,1024]{2,1,0:T(8,128)(2,1)S(1)}, u32[]{:S(2)}, u32[]{:S(2)}) %collective-permute-start.7) | collective-permute-done | bytes 524320 | tf_op jit(solution)/shard_map/ppermute | solution.py:139
  61.3 2.5 %collective-permute-start.8 = (bf16[2,64,1024]{2,1,0:T(8,128)(2,1)S(1)}, bf16[2,64,1024]{2,1,0:T(8,128)(2,1)S(1)}, u32[]{:S(2)}, u32[]{:S(2)}) collective-permute-start(bf16[2,64,1024]{2,1,0:T(8,128)(2,1)S(1)} %slice.8), channel_id=1, source_target_pairs={{0,32},{16,48},{32,0},{48,16},{64,96},{80,112},{96,64},{112,80},{1... | collective-permute-start | bytes 786440 | tf_op jit(solution)/shard_map/ppermute | solution.py:140
  64.1 1.2 collective-permute-done.6
  65.4 1.0 slice.9
  66.3 3.3 %collective-permute-start.9 = (bf16[2,64,1024]{2,1,0:T(8,128)(2,1)S(1)}, bf16[2,64,1024]{2,1,0:T(8,128)(2,1)S(1)}, u32[]{:S(2)}, u32[]{:S(2)}) collective-permute-start(bf16[2,64,1024]{2,1,0:T(8,128)(2,1)S(1)} %slice.9), channel_id=1, source_target_pairs={{0,96},{16,112},{32,64},{48,80},{64,32},{80,48},{96,0},{112,16},{1... | collective-permute-start | bytes 786440 | tf_op jit(solution)/shard_map/ppermute | solution.py:141
  69.6 1.1 constant_dynamic-update-slice_fusion.5
  70.8 5.2 %collective-permute-done.9 = bf16[2,64,1024]{2,1,0:T(8,128)(2,1)S(1)} collective-permute-done((bf16[2,64,1024]{2,1,0:T(8,128)(2,1)S(1)}, bf16[2,64,1024]{2,1,0:T(8,128)(2,1)S(1)}, u32[]{:S(2)}, u32[]{:S(2)}) %collective-permute-start.9) | collective-permute-done | bytes 262176 | tf_op jit(solution)/shard_map/ppermute | solution.py:141
  76.1 11.5 %collective-permute-start.10 = (bf16[16,64,1024]{2,1,0:T(8,128)(2,1)S(1)}, bf16[16,64,1024]{2,1,0:T(8,128)(2,1)}, u32[]{:S(2)}, u32[]{:S(2)}) collective-permute-start(bf16[16,64,1024]{2,1,0:T(8,128)(2,1)S(1)} %constant_dynamic-update-slice_fusion.2), channel_id=1, source_target_pairs={{0,16},{16,0},{32,48},{48,32},{64,80},{80,64},{96,112},{112,96},{1... | collective-permute-start | bytes 6291464 | tf_op jit(solution)/shard_map/ppermute | solution.py:145
  87.6 0.5 broadcast_in_dim.27
  88.1 0.3 constant_dynamic-update-slice_fusion.1
  88.4 3.0 %collective-permute-done.10 = bf16[16,64,1024]{2,1,0:T(8,128)(2,1)} collective-permute-done((bf16[16,64,1024]{2,1,0:T(8,128)(2,1)S(1)}, bf16[16,64,1024]{2,1,0:T(8,128)(2,1)}, u32[]{:S(2)}, u32[]{:S(2)}) %collective-permute-start.10) | collective-permute-done | bytes 2097184 | tf_op jit(solution)/shard_map/ppermute | solution.py:145
  91.5 1.9 %constant_dynamic-update-slice_fusion = bf16[32,64,1024]{2,1,0:T(8,128)(2,1)S(1)} fusion(bf16[32,64,1024]{2,1,0:T(8,128)(2,1)S(1)} %constant_dynamic-update-slice_fusion.1, bf16[16,64,1024]{2,1,0:T(8,128)(2,1)} %collective-permute-done.10, s32[]{:T(128)S(6)} %select_n.65), kind=kLoop, calls=%fused_computation.7 | loop fusion | bytes 4194308 | tf_op jit(solution)/shard_map/dynamic_update_slice | solution.py:148
  93.4 1.9 %copy-done.1 = bf16[32,64,1024]{2,1,0:T(8,128)(2,1)} copy-done((bf16[32,64,1024]{2,1,0:T(8,128)(2,1)}, bf16[32,64,1024]{2,1,0:T(8,128)(2,1)S(1)}, u32[]{:S(2)}) %copy-start.1) | copy-done | bytes 4194328
  95.3 6.4 %copy.7 = bf16[4,512,1024]{1,2,0:T(8,128)(2,1)} copy(bf16[4,512,1024]{2,1,0:T(8,128)(2,1)} %bitcast.14) | data formatting | bytes 8388608 | tf_op jit(solution)/shard_map/reshape | solution.py:149
  101.7 21.9 %all-gather.3.cloned.1.call-done = bf16[16384,256]{1,0:T(8,128)(2,1)} async-done(((bf16[1024,256]{1,0:T(8,128)(2,1)}), bf16[16384,256]{1,0:T(8,128)(2,1)}) %all-gather.3.cloned.1.call-update) | async-done | bytes 8388624 | tf_op jit(solution)/shard_map/all_gather | solution.py:129
  123.7 7.5 %shard_map.68 = (bf16[1024,512]{1,0:T(8,128)(2,1)S(1)}, f32[16,8,128]{2,1,0:T(8,128)}) custom-call(s32[1]{0:T(128)} %bitcast.z_ref, bf16[1024,512]{1,0:T(8,128)(2,1)S(1)} %copy-done, bf16[4,1024,512]{2,1,0:T(8,128)(2,1)} %bitcast.15, bf16[16,1024,256]{2,1,0:T(8,128)(2,1)} %bitcast.16), custom_call_target="tpu_custom_call" | custom-call | flops 4294967296 | bytes 14680064 | tf_op jit(solution)/shard_map/pallas_call | solution.py:97
  131.2 9.7 %all-to-all-start = ((f32[16,8,128]{2,1,0:T(8,128)}), f32[16,8,128]{2,1,0:T(8,128)S(1)}, u32[]{:S(2)}, u32[]{:S(2)}) async-start(f32[16,8,128]{2,1,0:T(8,128)} %get-tuple-element.5), calls=%async_computation | async-start | bytes 131072 | tf_op jit(solution)/shard_map/all_to_all | solution.py:152
  140.9 13.0 %all-to-all-done = f32[16,8,128]{2,1,0:T(8,128)S(1)} async-done(((f32[16,8,128]{2,1,0:T(8,128)}), f32[16,8,128]{2,1,0:T(8,128)S(1)}, u32[]{:S(2)}, u32[]{:S(2)}) %all-to-all-start) | async-done | bytes 65568 | tf_op jit(solution)/shard_map/all_to_all | solution.py:152
  153.9 1.3 multiply_convert_fusion
  (24 shorter events, 0.6 us)
Async XLA Ops:
  7.2 116.5 %all-gather.3.cloned.1.call-start = ((), (), s32[]{:S(2)}) async-start(), calls=%async_computation.1 | async-start | bytes 8912896 | tf_op jit(solution)/shard_map/all_gather | solution.py:129
  9.6 10.8 %collective-permute-start = (bf16[64,1024]{1,0:T(8,128)(2,1)S(1)}, bf16[64,1024]{1,0:T(8,128)(2,1)S(1)}, u32[]{:S(2)}, u32[]{:S(2)}) collective-permute-start(bf16[64,1024]{1,0:T(8,128)(2,1)S(1)} %get-tuple-element.6), channel_id=1, source_target_pairs={{0,0},{4,84},{8,24},{12,76},{16,128},{20,212},{24,152},{28,204},{3... | collective-permute-start | bytes 393224 | tf_op jit(solution)/shard_map/ppermute | solution.py:132
  20.4 0.7 collective-permute-start.1
  21.1 0.7 collective-permute-start.2
  21.8 9.3 %collective-permute-start.3 = (bf16[64,1024]{1,0:T(8,128)(2,1)S(1)}, bf16[64,1024]{1,0:T(8,128)(2,1)S(1)}, u32[]{:S(2)}, u32[]{:S(2)}) collective-permute-start(bf16[64,1024]{1,0:T(8,128)(2,1)S(1)} %collective-permute-done.2), channel_id=1, source_target_pairs={{0,128},{16,144},{32,160},{48,176},{64,192},{80,208},{96,224},{112... | collective-permute-start | bytes 393224 | tf_op jit(solution)/shard_map/ppermute | solution.py:136
  25.1 8.5 %collective-permute-start.4 = (bf16[64,1024]{1,0:T(8,128)(2,1)S(1)}, bf16[64,1024]{1,0:T(8,128)(2,1)S(1)}, u32[]{:S(2)}, u32[]{:S(2)}) collective-permute-start(bf16[64,1024]{1,0:T(8,128)(2,1)S(1)} %collective-permute-done.2), channel_id=1, source_target_pairs={{0,256},{16,272},{32,288},{48,304},{64,320},{80,336},{96,352},{112... | collective-permute-start | bytes 393224 | tf_op jit(solution)/shard_map/ppermute | solution.py:136
  27.0 7.8 %collective-permute-start.5 = (bf16[64,1024]{1,0:T(8,128)(2,1)S(1)}, bf16[64,1024]{1,0:T(8,128)(2,1)S(1)}, u32[]{:S(2)}, u32[]{:S(2)}) collective-permute-start(bf16[64,1024]{1,0:T(8,128)(2,1)S(1)} %collective-permute-done.2), channel_id=1, source_target_pairs={{0,384},{16,400},{32,416},{48,432},{64,448},{80,464},{96,480},{112... | collective-permute-start | bytes 393224 | tf_op jit(solution)/shard_map/ppermute | solution.py:136
  34.8 26.5 %collective-permute-start.7 = (bf16[4,64,1024]{2,1,0:T(8,128)(2,1)S(1)}, bf16[4,64,1024]{2,1,0:T(8,128)(2,1)S(1)}, u32[]{:S(2)}, u32[]{:S(2)}) collective-permute-start(bf16[4,64,1024]{2,1,0:T(8,128)(2,1)S(1)} %bitcast_dynamic-update-slice_fusion), channel_id=1, source_target_pairs={{0,96},{16,112},{32,64},{48,80},{64,32},{80,48},{96,0},{112,16},{1... | collective-permute-start | bytes 1572872 | tf_op jit(solution)/shard_map/ppermute | solution.py:139
  54.2 11.2 %collective-permute-start.6 = (bf16[4,64,1024]{2,1,0:T(8,128)(2,1)S(1)}, bf16[4,64,1024]{2,1,0:T(8,128)(2,1)}, u32[]{:S(2)}, u32[]{:S(2)}) collective-permute-start(bf16[4,64,1024]{2,1,0:T(8,128)(2,1)S(1)} %bitcast_dynamic-update-slice_fusion), channel_id=1, source_target_pairs={{0,32},{16,48},{32,0},{48,16},{64,96},{80,112},{96,64},{112,80},{1... | collective-permute-start | bytes 1572872 | tf_op jit(solution)/shard_map/ppermute | solution.py:138
  61.3 9.5 %collective-permute-start.8 = (bf16[2,64,1024]{2,1,0:T(8,128)(2,1)S(1)}, bf16[2,64,1024]{2,1,0:T(8,128)(2,1)S(1)}, u32[]{:S(2)}, u32[]{:S(2)}) collective-permute-start(bf16[2,64,1024]{2,1,0:T(8,128)(2,1)S(1)} %slice.8), channel_id=1, source_target_pairs={{0,32},{16,48},{32,0},{48,16},{64,96},{80,112},{96,64},{112,80},{1... | collective-permute-start | bytes 786440 | tf_op jit(solution)/shard_map/ppermute | solution.py:140
  66.3 9.7 %collective-permute-start.9 = (bf16[2,64,1024]{2,1,0:T(8,128)(2,1)S(1)}, bf16[2,64,1024]{2,1,0:T(8,128)(2,1)S(1)}, u32[]{:S(2)}, u32[]{:S(2)}) collective-permute-start(bf16[2,64,1024]{2,1,0:T(8,128)(2,1)S(1)} %slice.9), channel_id=1, source_target_pairs={{0,96},{16,112},{32,64},{48,80},{64,32},{80,48},{96,0},{112,16},{1... | collective-permute-start | bytes 786440 | tf_op jit(solution)/shard_map/ppermute | solution.py:141
  76.1 15.4 %collective-permute-start.10 = (bf16[16,64,1024]{2,1,0:T(8,128)(2,1)S(1)}, bf16[16,64,1024]{2,1,0:T(8,128)(2,1)}, u32[]{:S(2)}, u32[]{:S(2)}) collective-permute-start(bf16[16,64,1024]{2,1,0:T(8,128)(2,1)S(1)} %constant_dynamic-update-slice_fusion.2), channel_id=1, source_target_pairs={{0,16},{16,0},{32,48},{48,32},{64,80},{80,64},{96,112},{112,96},{1... | collective-permute-start | bytes 6291464 | tf_op jit(solution)/shard_map/ppermute | solution.py:145
  93.4 1.9 %copy-start.1 = (bf16[32,64,1024]{2,1,0:T(8,128)(2,1)}, bf16[32,64,1024]{2,1,0:T(8,128)(2,1)S(1)}, u32[]{:S(2)}) copy-start(bf16[32,64,1024]{2,1,0:T(8,128)(2,1)S(1)} %constant_dynamic-update-slice_fusion) | copy-start | bytes 12582916
  95.3 28.3 %copy-start = (bf16[1024,512]{1,0:T(8,128)(2,1)S(1)}, bf16[1024,512]{1,0:T(8,128)(2,1)}, u32[]{:S(2)}) copy-start(bf16[1024,512]{1,0:T(8,128)(2,1)} %base.1) | copy-start | bytes 3145732
  123.7 17.2 %copy-start.2 = (bf16[512]{0:T(512)(128)(2,1)S(1)}, bf16[512]{0:T(512)(128)(2,1)}, u32[]{:S(2)}) copy-start(bf16[512]{0:T(512)(128)(2,1)} %param.9) | copy-start | bytes 3076
  131.2 22.7 %all-to-all-start = ((f32[16,8,128]{2,1,0:T(8,128)}), f32[16,8,128]{2,1,0:T(8,128)S(1)}, u32[]{:S(2)}, u32[]{:S(2)}) async-start(f32[16,8,128]{2,1,0:T(8,128)} %get-tuple-element.5), calls=%async_computation | async-start | bytes 131072 | tf_op jit(solution)/shard_map/all_to_all | solution.py:152
Sparse Core Ops, SparseCore 0:
  10.1 113.5 all-gather.2
